TPU v7x, 32 devices: a whole 2x2x4 slice. The times are simulated.
32 devices in a mesh: pts: 16 (over z, y, core), freq: 2 (over x).
Axes of the slice: x: 2, y: 2, z: 4, core: 2. Of those that a mesh axis runs over, the one named last changes fastest.
Arguments:
- snapshots: float32 [2112, 12288], P(None, ('pts', 'freq')), may hold values from -6 to 6
- weight: float32 [12288], P('pts'), may hold values from 0.1 to 10
- start_vec: float32 [64, 2, 32], replicated, may hold values from -6 to 6
Outputs:
- gram_mine: float32 [64, 2, 32, 32], P('freq')
- modes: float32 [64, 2, 12288], P('freq', None, 'pts')
All inputs are finite; a program needn't handle non-finite values.
Results may differ from a plain program's by a relative error of at most 0.0003.
Values sent between devices are 32-bit elements; how exact they have to be, the bound alone decides.
No kernel may reach another device: no remote copies, remote signals or barrier semaphores. Data moves between devices by JAX's collectives and lax.ppermute only.
A program may use at most 64 MiB of HBM per device.

v0:
```python
import functools
import math

import jax
import jax.numpy as jnp
import numpy as np
from jax import lax
from jax.experimental import pallas as pl
from jax.experimental.pallas import tpu as pltpu
from jax.sharding import PartitionSpec as P

NFFT = 128
HALF = NFFT // 2
NF = 64
NB = 32
LANES = 128
PACK = 4
VMEM_LIMIT = 51 * 1024 * 1024
SMALL_LIMIT = 8 * 1024 * 1024
VMEM = pl.BlockSpec(memory_space=pltpu.VMEM)


def dft_values():
    times = np.arange(NFFT)
    freqs = np.arange(NF)
    phases = (freqs[:, None] * times[None, :] % NFFT) * (2.0 * math.pi / NFFT)
    window = 0.5 - 0.5 * np.cos(times * (2.0 * math.pi / NFFT))
    weighted = window / np.sqrt(np.sum(window * window))
    return np.cos(phases) * weighted, -np.sin(phases) * weighted


def split_table(table):
    high = table.astype(jnp.bfloat16)
    low = (table - high.astype(np.float64)).astype(jnp.bfloat16)
    return high, low


def mode_tables():
    real, imag = dft_values()
    order = np.arange(NF).reshape(NF // PACK, PACK).T
    real, imag = real[order], imag[order]
    first = np.stack([real, imag], axis=1).reshape(2 * NF, NFFT)
    second = np.stack([-imag, real], axis=1).reshape(2 * NF, NFFT)
    return np.stack([first, second]).astype(np.float32)


def cosine_of_turns(count):
    folded = jnp.minimum(count, NFFT - count)
    angle = (NFFT // 4 - folded).astype(jnp.float32) * (2.0 * math.pi / NFFT)
    square = angle * angle
    series = 1.0
    for n in (10, 8, 6, 4, 2):
        series = 1.0 - square * series * (1.0 / (n * (n + 1)))
    return angle * series


def fill_dft(dft_ref):
    row = lax.broadcasted_iota(jnp.int32, (2 * NF, NFFT), 0)
    time = lax.broadcasted_iota(jnp.int32, (2 * NF, NFFT), 1)
    quarter = jnp.where(row < NF, 0, NFFT // 4)
    wave = cosine_of_turns((row % NF * time + quarter) % NFFT)
    window = 0.5 - 0.5 * np.cos(np.arange(NFFT) * (2.0 * math.pi / NFFT))
    norm = float(np.sqrt(np.sum(window * window)))
    high, low = split(wave * ((0.5 - 0.5 * cosine_of_turns(time)) / norm))
    dft_ref[pl.ds(0, 2 * NF), pl.ds(0, NFFT)] = high
    dft_ref[pl.ds(0, 2 * NF), pl.ds(NFFT, NFFT)] = high
    dft_ref[pl.ds(2 * NF, 2 * NF), pl.ds(0, NFFT)] = low
    dft_ref[pl.ds(2 * NF, 2 * NF), pl.ds(NFFT, NFFT)] = jnp.zeros((2 * NF, NFFT), jnp.bfloat16)


def spread_start(start_ref, spread_ref):
    row = lax.broadcasted_iota(jnp.int32, (NF, LANES), 0)
    lane = lax.broadcasted_iota(jnp.int32, (NF, LANES), 1)
    start = start_ref[pl.ds(0, 2 * NB), pl.ds(0, NF)]
    for g in range(NF // PACK):
        pick = (row == PACK * g + lane // NB).astype(jnp.float32)
        spread_ref[g] = jnp.dot(
            start,
            pick,
            precision=lax.Precision.HIGHEST,
            preferred_element_type=jnp.float32,
        )


def split(value):
    high = value.astype(jnp.bfloat16)
    low = (value - high.astype(jnp.float32)).astype(jnp.bfloat16)
    return high, low


def load_weights(w_ref, col_tiles):
    first = lax.axis_index("freq") * col_tiles
    return jnp.concatenate([w_ref[pl.ds(first + c, 1), :] for c in range(col_tiles)], axis=1)


def flip_groups(groups, flipped):
    turned = flipped.T
    lane = lax.broadcasted_iota(jnp.int32, (NB, LANES), 1)
    out = []
    for g in range(PACK):
        total = groups[g]
        for q in range(PACK):
            block = turned[q * NB : (q + 1) * NB]
            if q != g:
                block = pltpu.roll(block, ((q - g) % PACK) * NB, 1)
            total = total + jnp.where(lane // NB == q, block, 0.0)
        out.append(total)
    return out


ROW_STEP = 3
FREQ_STEP = ROW_STEP * NB + 1


def core_bit():
    return lax.rem(lax.axis_index("pts"), 2)


def y_bit():
    return lax.rem(lax.div(lax.axis_index("pts"), 2), 2)


RESP_ROWS = 2 * NF // PACK


def give_half(value_ref, bit, keep_ref, send_ref):
    half = keep_ref.shape[0] - RESP_ROWS
    keep_ref[pl.ds(0, half), :] = value_ref[pl.ds(bit * half, half), :]
    send_ref[pl.ds(0, half), :] = value_ref[pl.ds((1 - bit) * half, half), :]
    resp = value_ref[pl.ds(2 * half, RESP_ROWS), :]
    keep_ref[pl.ds(half, RESP_ROWS), :] = resp
    send_ref[pl.ds(half, RESP_ROWS), :] = resp


def gram_kernel(
    total_rows,
    places,
    by_core,
    x_hbm,
    aux_ref,
    keep_ref,
    send_ref,
    high_ref,
    low_hbm,
    x_ref,
    dft_ref,
    low_ref,
    spec_ref,
    z_even,
    z_odd,
    real_ref,
    imag_ref,
    spread_ref,
    pack_ref,
    in_sems,
    out_sem,
):
    times, cols = x_ref.shape
    halves = times // HALF
    col_tiles = cols // LANES
    pieces = in_sems.shape[0]
    piece = times // pieces

    def fetch(i):
        rows = pl.ds(i * piece, piece)
        return pltpu.make_async_copy(x_hbm.at[rows], x_ref.at[rows], in_sems.at[i])

    for i in range(pieces):
        fetch(i).start()
    fill_dft(dft_ref)
    spread_start(aux_ref, spread_ref)

    acc = jnp.zeros((HALF, cols), jnp.float32)
    for i in range(pieces):
        fetch(i).wait()
        for h in range(piece // HALF):
            acc = acc + x_ref[pl.ds(i * piece + h * HALF, HALF), :]
    mean = jnp.sum(acc, axis=0, keepdims=True) / times
    weights = load_weights(aux_ref.at[pl.ds(2 * NB, aux_ref.shape[0] - 2 * NB)], col_tiles)
    scale = jnp.sqrt(weights / (2.0 * total_rows))

    def center(i, carry):
        rows = pl.ds(pl.multiple_of(i * HALF, HALF), HALF)
        high, low = split((x_ref[rows, :] - mean) * scale)
        high_ref[rows, :] = high
        low_ref[rows, :] = low
        return carry

    lax.fori_loop(0, halves, center, 0, unroll=3)
    pad = high_ref.shape[0] - times
    if pad:
        high_ref[pl.ds(times, pad), :] = jnp.zeros((pad, cols), jnp.bfloat16)
        low_ref[pl.ds(times, pad), :] = jnp.zeros((pad, cols), jnp.bfloat16)
    save_low = pltpu.make_async_copy(low_ref, low_hbm, out_sem)
    save_low.start()

    def transform(i, carry):
        blocks = []
        for s in range(2):
            rows = pl.ds(pl.multiple_of((2 * i + s) * HALF, HALF), NFFT)
            blocks.append(jnp.concatenate([high_ref[rows, :], low_ref[rows, :]], axis=0))
        both = jnp.dot(
            dft_ref[...], jnp.concatenate(blocks, axis=1), preferred_element_type=jnp.float32
        )
        spectrum = both[: 2 * NF] + both[2 * NF :]
        for s in range(2):
            for o in range(2 * NF // 8):
                for c in range(col_tiles):
                    first = s * cols + c * LANES
                    rows = pl.ds(ROW_STEP * (2 * i + s), 8, stride=FREQ_STEP)
                    spec_ref[c, o, rows, :] = spectrum[8 * o : 8 * o + 8, first : first + LANES]
        return carry

    lax.fori_loop(0, NB // 2, transform, 0, unroll=2)

    row = lax.broadcasted_iota(jnp.int32, (NB, LANES), 0)
    lane = lax.broadcasted_iota(jnp.int32, (NB, LANES), 1)
    upper = row <= lane % NB
    octets = NF // 8

    def prepare(z_ref, octet, half):
        for part in range(2):
            for q in range(PACK):
                rows = pl.ds(FREQ_STEP * (PACK * half + q), NB, stride=ROW_STEP)
                own = pl.ds(part * LANES + q * NB, NB)
                for c in range(col_tiles):
                    value = spec_ref[c, octet + octets * part, rows, :]
                    high = value.astype(jnp.bfloat16)
                    low = (2.0 * (value - high.astype(jnp.float32))).astype(jnp.bfloat16)
                    z_ref[own, pl.ds(c * LANES, LANES)] = high
                    z_ref[own, pl.ds(cols + c * LANES, LANES)] = low

    def correlate(z_ref, group):
        high = z_ref[:, pl.ds(0, cols)]
        product = lax.dot_general(
            jnp.concatenate([high, high], axis=1),
            z_ref[...],
            (((1,), (1,)), ((), ())),
            preferred_element_type=jnp.float32,
        )
        gram_real = jnp.zeros((NB, LANES), jnp.float32)
        gram_imag = jnp.zeros((NB, LANES), jnp.float32)
        for q in range(PACK):
            mine = lane // NB == q
            real = product[q * NB : (q + 1) * NB]
            imag = product[LANES + q * NB : LANES + (q + 1) * NB]
            gram_real = jnp.where(mine, real[:, :LANES] + imag[:, LANES:], gram_real)
            gram_imag = jnp.where(mine, real[:, LANES:] - imag[:, :LANES], gram_imag)
        real_ref[group] = gram_real
        imag_ref[group] = gram_imag

    prepare(z_even, 0, 0)

    def step(o, carry):
        prepare(z_odd, o, 1)
        correlate(z_even, 2 * o)
        prepare(z_even, jnp.minimum(o + 1, octets - 1), 0)
        correlate(z_odd, 2 * o + 1)
        return carry

    lax.fori_loop(0, octets, step, 0)
    left = lane[: NB // 2] < LANES // 2
    half = NB // 2
    resp_real = []
    resp_imag = []
    for quad in range(NF // PACK // PACK):
        own = pl.ds(quad * PACK, PACK)
        reals = [real_ref[quad * PACK + g] for g in range(PACK)]
        imags = [imag_ref[quad * PACK + g] for g in range(PACK)]
        reals = flip_groups(reals, real_ref[own].reshape(PACK * NB, LANES))
        imags = flip_groups(imags, -imag_ref[own].reshape(PACK * NB, LANES))
        for g, (real, imag) in enumerate(zip(reals, imags)):
            group = quad * PACK + g
            start_real = spread_ref[group, pl.ds(0, NB), :]
            start_imag = spread_ref[group, pl.ds(NB, NB), :]
            resp_real.append(
                jnp.sum(real * start_real + imag * start_imag, axis=0, keepdims=True)
            )
            resp_imag.append(
                jnp.sum(real * start_imag - imag * start_real, axis=0, keepdims=True)
            )
            packed = jnp.where(upper, real, imag)
            top = packed[:half]
            bottom = packed[half:]
            even = jnp.where(left, top, pltpu.roll(bottom, LANES // 2, 1))
            odd = jnp.where(left, pltpu.roll(top, LANES // 2, 1), bottom)
            pack_ref[pl.ds(places[2 * group] * half, half), :] = even
            pack_ref[pl.ds(places[2 * group + 1] * half, half), :] = odd
    resp = jnp.concatenate(resp_real + resp_imag, axis=0)
    pack_ref[pl.ds(NF // 2 * half, RESP_ROWS), :] = resp
    give_half(pack_ref, core_bit() if by_core else 0, keep_ref, send_ref)
    save_low.wait()


def gram_parts(snapshots, weight_rows, start_vec, total_rows, places, by_core):
    times, cols = snapshots.shape
    start = jnp.transpose(start_vec, (1, 2, 0)).reshape(2 * NB, NF)
    start = jnp.pad(start, ((0, 0), (0, LANES - NF)))
    aux = jnp.concatenate([start, weight_rows], axis=0)
    pieces = 11
    any_space = pl.BlockSpec(memory_space=pl.ANY)
    saved = jax.ShapeDtypeStruct((-(-times // LANES) * LANES, cols), jnp.bfloat16)
    half = floats(NF // 4 * NB // 2 + RESP_ROWS, LANES)
    return pl.pallas_call(
        functools.partial(gram_kernel, total_rows, places, by_core),
        out_shape=(half, half, saved, saved),
        in_specs=[any_space, VMEM],
        out_specs=(VMEM, VMEM, VMEM, any_space),
        scratch_shapes=[
            pltpu.VMEM((times, cols), jnp.float32),
            pltpu.VMEM((4 * NF, 2 * NFFT), jnp.bfloat16),
            pltpu.VMEM(saved.shape, jnp.bfloat16),
            pltpu.VMEM((cols // LANES, 2 * NF // 8, 8 * FREQ_STEP, LANES), jnp.float32),
            pltpu.VMEM((2 * LANES, 2 * cols), jnp.bfloat16),
            pltpu.VMEM((2 * LANES, 2 * cols), jnp.bfloat16),
            pltpu.VMEM((NF // PACK, NB, LANES), jnp.float32),
            pltpu.VMEM((NF // PACK, NB, LANES), jnp.float32),
            pltpu.VMEM((NF // PACK, 2 * NB, LANES), jnp.float32),
            pltpu.VMEM((NF // 2 * NB // 2 + RESP_ROWS, LANES), jnp.float32),
            pltpu.SemaphoreType.DMA((pieces,)),
            pltpu.SemaphoreType.DMA(()),
        ],
        compiler_params=pltpu.CompilerParams(vmem_limit_bytes=VMEM_LIMIT),
        cost_estimate=pl.CostEstimate(
            flops=5_000_000_000, bytes_accessed=8_000_000, transcendentals=0
        ),
        name="gram_parts",
    )(snapshots, aux)


def pair_square(even, odd):
    left = lax.broadcasted_iota(jnp.int32, (NB // 2, LANES), 1) < LANES // 2
    top = jnp.where(left, even, pltpu.roll(odd, LANES // 2, 1))
    bottom = jnp.where(left, pltpu.roll(even, LANES // 2, 1), odd)
    return jnp.concatenate([top, bottom], axis=0)


def hermitian(squares):
    row = lax.broadcasted_iota(jnp.int32, (NB, LANES), 0)
    col = lax.broadcasted_iota(jnp.int32, (NB, LANES), 1) % NB
    zero = jnp.zeros((NB, LANES), jnp.float32)
    full = squares + [zero] * (PACK - len(squares))
    turned = flip_groups([zero] * PACK, jnp.concatenate(full, axis=0))
    for square, flipped in zip(squares, turned):
        real = jnp.where(row <= col, square, flipped)
        imag = jnp.where(row > col, square, jnp.where(row < col, -flipped, 0.0))
        yield real, imag


def small_call(kernel, name, out_shape, scratch_shapes=(), limit=SMALL_LIMIT):
    def call(*args):
        return pl.pallas_call(
            kernel,
            out_shape=out_shape,
            in_specs=[VMEM] * len(args),
            out_specs=VMEM if isinstance(out_shape, jax.ShapeDtypeStruct) else (VMEM,) * len(out_shape),
            scratch_shapes=list(scratch_shapes),
            compiler_params=pltpu.CompilerParams(vmem_limit_bytes=limit),
            name=name,
        )(*args)

    return call


def floats(*shape):
    return jax.ShapeDtypeStruct(shape, jnp.float32)


def add_core_kernel(kept_ref, got_ref, out_ref):
    quarter = out_ref.shape[1] - RESP_ROWS
    tail = pl.ds(4 * quarter, RESP_ROWS)
    resp = kept_ref[tail, :] + got_ref[tail, :]
    for m in range(4):
        rows = pl.ds(m * quarter, quarter)
        out_ref[m, pl.ds(0, quarter), :] = kept_ref[rows, :] + got_ref[rows, :]
        out_ref[m, pl.ds(quarter, RESP_ROWS), :] = resp


def add_core(kept, got):
    quarter = (kept.shape[0] - RESP_ROWS) // 4
    return small_call(add_core_kernel, "add_core", floats(4, quarter + RESP_ROWS, LANES))(kept, got)


def add_near_kernel(parts_ref, out_ref):
    out_ref[...] = (parts_ref[0] + parts_ref[1]) + (parts_ref[2] + parts_ref[3])


def add_kernel(kept_ref, got_ref, out_ref):
    out_ref[...] = kept_ref[...] + got_ref[...]


def add(name, kept, got):
    return small_call(add_kernel, name, floats(*kept.shape))(kept, got)


def finish_kernel(kept_ref, got_ref, packed_ref, resp_ref):
    rows = packed_ref.shape[0]
    packed_ref[...] = kept_ref[pl.ds(0, rows), :] + got_ref[pl.ds(0, rows), :]
    tail = pl.ds(rows, RESP_ROWS)
    resp = kept_ref[tail, :] + got_ref[tail, :]
    real = resp[: RESP_ROWS // 2]
    imag = resp[RESP_ROWS // 2 :]
    power = real * real + imag * imag
    lane = lax.broadcasted_iota(jnp.int32, power.shape, 1)
    mean = jnp.zeros(power.shape, jnp.float32)
    for q in range(PACK):
        mine = lane // NB == q
        part = jnp.sum(jnp.where(mine, power, 0.0), axis=1, keepdims=True) / NB
        mean = jnp.where(mine, part, mean)
    scaling = 1.0 / jnp.sqrt(mean + 1e-06)
    resp_ref[pl.ds(0, RESP_ROWS // 2), :] = real * scaling
    resp_ref[pl.ds(RESP_ROWS // 2, RESP_ROWS // 2), :] = imag * scaling


def finish(kept, got):
    rows = kept.shape[0] - RESP_ROWS
    return small_call(finish_kernel, "finish", (floats(rows, LANES), floats(RESP_ROWS, LANES)))(
        kept, got
    )


def join_y_kernel(own_ref, got_ref, packed_ref):
    rows = own_ref.shape[0]
    for m, ref in enumerate((own_ref, got_ref)):
        packed_ref[pl.ds((y_bit() ^ m) * rows, rows), :] = ref[...]


def unpack_kernel(*refs):
    parts, out_ref = refs[:-1], refs[-1]
    half = NB // 2
    for m, part in enumerate(parts):
        count = part.shape[0] // half
        place = (core_bit() ^ m) * 2 * count if len(parts) > 1 else 0
        for first in range(0, count, 2 * PACK):
            last = min(first + 2 * PACK, count)
            pairs = [part[pl.ds(i * half, half), :] for i in range(first, last)]
            squares = [pair_square(*pairs[i : i + 2]) for i in range(0, len(pairs), 2)]
            for g, both in enumerate(hermitian(squares)):
                for q in range(PACK):
                    freq = place + 2 * first + PACK * g + q
                    for c in range(2):
                        out_ref[freq, c] = both[c][:, q * NB : (q + 1) * NB]


def unpack_gram(*parts):
    count = sum(part.shape[0] for part in parts) * 4 // NB
    return small_call(unpack_kernel, "unpack_gram", floats(count, 2, NB, NB))(*parts)


def modes_kernel(
    total_rows, high_ref, low_hbm, w_ref, table_ref, resp_ref, out_ref, low_ref, a_ref, sem
):
    padded, cols = high_ref.shape
    fetch_low = pltpu.make_async_copy(low_hbm, low_ref, sem)
    fetch_low.start()
    groups = RESP_ROWS // 2
    lane = lax.broadcasted_iota(jnp.int32, (RESP_ROWS, LANES), 1)
    left = lane < HALF
    for q in range(PACK):
        resp = resp_ref[...]
        if q:
            resp = pltpu.roll(resp, LANES - q * NB, 1)
        real = jnp.concatenate([resp[:groups]] * 2, axis=0)
        imag = jnp.concatenate([resp[groups:]] * 2, axis=0)
        rows = pl.ds(q * RESP_ROWS, RESP_ROWS)
        first = table_ref[0, rows, :]
        second = table_ref[1, rows, :]
        first_turned = pltpu.roll(first, HALF, 1)
        second_turned = pltpu.roll(second, HALF, 1)

        def spread(value, block):
            if 0 <= block < NB:
                return jnp.broadcast_to(value[:, block : block + 1], (RESP_ROWS, LANES))
            return jnp.zeros((RESP_ROWS, LANES), jnp.float32)

        for m in range(padded // LANES):
            value = first_turned * jnp.where(left, spread(real, 2 * m - 1), spread(real, 2 * m + 1))
            value += second_turned * jnp.where(
                left, spread(imag, 2 * m - 1), spread(imag, 2 * m + 1)
            )
            if 2 * m < NB:
                value += first * spread(real, 2 * m) + second * spread(imag, 2 * m)
            high, low = split(value)
            own = pl.ds(m * LANES, LANES)
            a_ref[rows, own] = high
            a_ref[pl.ds(2 * NF + q * RESP_ROWS, RESP_ROWS), own] = low
    both = jnp.dot(a_ref[...], high_ref[...], preferred_element_type=jnp.float32)
    modes = both[: 2 * NF] + both[2 * NF :]
    fetch_low.wait()
    modes += jnp.dot(
        a_ref[pl.ds(0, 2 * NF), :], low_ref[...], preferred_element_type=jnp.float32
    )
    modes = modes * jnp.sqrt(2.0 * total_rows / load_weights(w_ref, cols // LANES))
    n_freq = out_ref.shape[0]
    mine = groups // n_freq
    group = lax.axis_index("freq")
    for q in range(PACK):
        for part in range(2):
            for f in range(n_freq):
                first = q * RESP_ROWS + part * groups + f * mine
                slot = f ^ group if n_freq == 2 else f
                for c in range(cols // LANES):
                    out_ref[slot, 2 * c + part, pl.ds(q, mine, stride=PACK), :] = modes[
                        first : first + mine, c * LANES : (c + 1) * LANES
                    ]


def local_modes(high, low, weight_rows, response, total_rows, n_freq):
    padded, cols = high.shape
    return pl.pallas_call(
        functools.partial(modes_kernel, total_rows),
        out_shape=floats(n_freq, 2 * cols // LANES, NF // n_freq, LANES),
        in_specs=[VMEM, pl.BlockSpec(memory_space=pl.ANY)] + [VMEM] * 3,
        out_specs=VMEM,
        scratch_shapes=[
            pltpu.VMEM((padded, cols), jnp.bfloat16),
            pltpu.VMEM((4 * NF, padded), jnp.bfloat16),
            pltpu.SemaphoreType.DMA(()),
        ],
        compiler_params=pltpu.CompilerParams(vmem_limit_bytes=VMEM_LIMIT),
        cost_estimate=pl.CostEstimate(
            flops=3_000_000_000, bytes_accessed=8_000_000, transcendentals=0
        ),
        name="local_modes",
    )(high, low, weight_rows, jnp.asarray(mode_tables()), response)


def join_kernel(kept_ref, got_ref, out_ref):
    tiles = got_ref.shape[0] // 2
    group = lax.axis_index("freq")
    for slot, ref in enumerate((kept_ref.at[0], got_ref)):
        for c in range(tiles):
            lanes = pl.ds(pl.multiple_of(((group ^ slot) * tiles + c) * LANES, LANES), LANES)
            for part in range(2):
                out_ref[:, part, lanes] = ref[2 * c + part]


def join_modes(kept, got):
    tiles, count, _ = got.shape
    return small_call(join_kernel, "join_modes", floats(count, 2, tiles * LANES))(kept, got)


def response_of(gram, start_vec):
    matvec = functools.partial(jnp.einsum, "fjk,fk->fj", precision=lax.Precision.HIGHEST)
    resp_real = matvec(gram[:, 0], start_vec[:, 0]) - matvec(gram[:, 1], start_vec[:, 1])
    resp_imag = matvec(gram[:, 0], start_vec[:, 1]) + matvec(gram[:, 1], start_vec[:, 0])
    scaling = 1.0 / jnp.sqrt(
        jnp.mean(resp_real * resp_real + resp_imag * resp_imag, axis=1, keepdims=True) + 1e-06
    )
    return jnp.stack([resp_real * scaling, resp_imag * scaling], axis=1)


def direction_shards(n_devices, snapshots, weight, start_vec):
    def swap(value, mask):
        return lax.ppermute(value, ("pts", "freq"), [(i, i ^ mask) for i in range(n_devices)])

    x, core, y, z_near, z_far = 1, 2, 4, 8, 16
    near = [
        [first + far, first + far + x, first + far + y, first + far + y + x]
        for far in range(0, n_devices, z_near)
        for first in (0, core)
    ]
    total_rows = float(weight.shape[0] * 16)
    weight_rows = weight.reshape(-1, LANES)
    places = [
        (i // 8 % 2) * 16 + (i // 4 % 2) * 8 + (i // 16) * 4 + i % 4 for i in range(NF // 2)
    ]
    keep, send, high, low = gram_parts(
        snapshots, weight_rows, start_vec, total_rows, places, True
    )
    parts = add_core(keep, swap(send, core))
    parts = lax.all_to_all(
        parts, ("pts", "freq"), 0, 0, axis_index_groups=near, tiled=True
    )
    part = small_call(add_near_kernel, "add_near", floats(*parts.shape[1:]))(parts)
    part = add("add_z", part, swap(part, z_near))
    packed, response = finish(part, swap(part, z_far))
    other = swap(packed, y)
    modes = local_modes(high, low, weight_rows, response, total_rows, 2)
    packed = small_call(join_y_kernel, "join_y", floats(2 * packed.shape[0], LANES))(packed, other)
    gram_mine = unpack_gram(packed, swap(packed, core))
    return gram_mine, join_modes(modes, swap(modes[1], x))


def shards(n_pts, n_freq, snapshots, weight, start_vec):
    cols = snapshots.shape[1]
    total_rows = float(weight.shape[0] * n_pts)
    n_devices = n_pts * n_freq
    mine_count = NF // n_freq
    group = lax.axis_index("freq")
    weight_rows = weight.reshape(-1, LANES)
    places = list(range(NF // 2))
    first, second, high, low = gram_parts(
        snapshots, weight_rows, start_vec, total_rows, places, False
    )
    parts = jnp.concatenate([first[:-RESP_ROWS], second[:-RESP_ROWS]], axis=0)
    share = parts.reshape(n_devices, -1)
    share = jnp.sum(lax.all_to_all(share, ("freq", "pts"), 0, 0, tiled=True), axis=0)
    packed = lax.all_gather(share, "pts", axis=0, tiled=True)
    gram_mine = unpack_gram(packed.reshape(-1, LANES))
    start_mine = lax.dynamic_slice_in_dim(start_vec, group * mine_count, mine_count, 0)
    response = lax.all_gather(response_of(gram_mine, start_mine), "freq", axis=0, tiled=True)
    response = jnp.transpose(response.reshape(NF // PACK, PACK, 2, NB), (2, 0, 1, 3))
    response = response.reshape(RESP_ROWS, LANES)
    modes = local_modes(high, low, weight_rows, response, total_rows, n_freq)
    modes = lax.all_to_all(modes, "freq", 0, 0, tiled=True)
    modes = modes.reshape(n_freq, cols // LANES, 2, mine_count, LANES)
    modes = jnp.transpose(modes, (3, 2, 0, 1, 4)).reshape(mine_count, 2, n_freq * cols)
    return gram_mine, modes


def solution(mesh):
    n_pts, n_freq = mesh.shape["pts"], mesh.shape["freq"]
    if (n_pts, n_freq) == (16, 2):
        body = functools.partial(direction_shards, n_pts * n_freq)
    else:
        body = functools.partial(shards, n_pts, n_freq)
    placed = (P(None, ("pts", "freq")), P("pts"), P())
    return jax.shard_map(
        body,
        mesh=mesh,
        in_specs=placed,
        out_specs=(P("freq", None, None, None), P("freq", None, "pts")),
        check_vma=False,
    )
```

profile of v0, /device:TPU:0, one launch (start us, length us, event | category | flops | bytes accessed | tf_op | source)
XLA Modules:
  0.0 42.8 jit_solution(4554910236243543802)
XLA Ops:
  0.6 0.8 %select_maximum_fusion.aux_ref = f32[70,128]{1,0:T(8,128)S(1)} fusion(f32[64,64]{1,0:T(8,128)} %bitcast.8, f32[6,128]{1,0:T(8,128)} %bitcast.6), kind=kLoop, calls=%fused_computation.1 | loop fusion | flops 26880 | bytes 55296 | tf_op jit(solution)/shard_map/concatenate | solution.py:299
  1.4 0.0 copy-start
  1.4 0.0 copy-start.1
  1.4 10.6 %gram_parts.1 = (f32[288,128]{1,0:T(8,128)S(1)}, f32[288,128]{1,0:T(8,128)S(1)}, bf16[2176,384]{1,0:T(8,128)(2,1)S(1)}, bf16[2176,384]{1,0:T(8,128)(2,1)}) custom-call(f32[2112,384]{1,0:T(8,128)} %x_hbm.1, f32[70,128]{1,0:T(8,128)S(1)} %select_maximum_fusion.aux_ref), custom_call_target="tpu_custom_call" | custom-call | flops 5000000000 | bytes 8000000 | tf_op jit(solution)/shard_map/gram_parts/pallas_call | solution.py:304
  12.0 0.5 %collective-permute-start = (f32[288,128]{1,0:T(8,128)S(1)}, f32[288,128]{1,0:T(8,128)S(1)}, u32[]{:S(2)}, u32[]{:S(2)}) collective-permute-start(f32[288,128]{1,0:T(8,128)S(1)} %get-tuple-element.9), channel_id=1, source_target_pairs={{0,2},{1,3},{2,0},{3,1},{4,6},{5,7},{6,4},{7,5},{8,10},{9,11},{10,... | collective-permute-start | bytes 442376 | tf_op jit(solution)/shard_map/ppermute | solution.py:555
  12.6 1.0 %collective-permute-done.got_ref = f32[288,128]{1,0:T(8,128)S(1)} collective-permute-done((f32[288,128]{1,0:T(8,128)S(1)}, f32[288,128]{1,0:T(8,128)S(1)}, u32[]{:S(2)}, u32[]{:S(2)}) %collective-permute-start) | collective-permute-done | bytes 147488 | tf_op jit(solution)/shard_map/ppermute | solution.py:555
  13.6 10.4 %all_to_all.5.parts_ref = f32[4,96,128]{2,1,0:T(8,128)S(1)} all-to-all(f32[4,96,128]{2,1,0:T(8,128)S(1)} %add_core.1), channel_id=1, replica_groups={{0,1,4,5},{2,3,6,7},{8,9,12,13},{10,11,14,15},{16,17,20,21},{18,19,22,2..., dimensions={0} | all-to-all | bytes 393216 | tf_op jit(solution)/shard_map/all_to_all | solution.py:572
  24.0 1.6 %collective-permute-start.1 = (f32[96,128]{1,0:T(8,128)S(1)}, f32[96,128]{1,0:T(8,128)S(1)}, u32[]{:S(2)}, u32[]{:S(2)}) collective-permute-start(f32[96,128]{1,0:T(8,128)S(1)} %add_near.1.kept_ref), channel_id=1, source_target_pairs={{0,8},{1,9},{2,10},{3,11},{4,12},{5,13},{6,14},{7,15},{8,0},{9,1},... | collective-permute-start | bytes 147464 | tf_op jit(solution)/shard_map/ppermute | solution.py:555
  25.7 2.5 %collective-permute-done.1.got_ref = f32[96,128]{1,0:T(8,128)S(1)} collective-permute-done((f32[96,128]{1,0:T(8,128)S(1)}, f32[96,128]{1,0:T(8,128)S(1)}, u32[]{:S(2)}, u32[]{:S(2)}) %collective-permute-start.1) | collective-permute-done | bytes 49184 | tf_op jit(solution)/shard_map/ppermute | solution.py:555
  28.2 2.6 %collective-permute-start.2 = (f32[96,128]{1,0:T(8,128)S(1)}, f32[96,128]{1,0:T(8,128)S(1)}, u32[]{:S(2)}, u32[]{:S(2)}) collective-permute-start(f32[96,128]{1,0:T(8,128)S(1)} %add_z.1.kept_ref), channel_id=1, source_target_pairs={{0,16},{1,17},{2,18},{3,19},{4,20},{5,21},{6,22},{7,23},{8,24},{9,... | collective-permute-start | bytes 147464 | tf_op jit(solution)/shard_map/ppermute | solution.py:555
  30.8 2.4 %collective-permute-done.2.got_ref = f32[96,128]{1,0:T(8,128)S(1)} collective-permute-done((f32[96,128]{1,0:T(8,128)S(1)}, f32[96,128]{1,0:T(8,128)S(1)}, u32[]{:S(2)}, u32[]{:S(2)}) %collective-permute-start.2) | collective-permute-done | bytes 49184 | tf_op jit(solution)/shard_map/ppermute | solution.py:555
  33.3 0.1 finish.1
  33.4 0.8 %collective-permute-start.3 = (f32[64,128]{1,0:T(8,128)S(1)}, f32[64,128]{1,0:T(8,128)S(1)}, u32[]{:S(2)}, u32[]{:S(2)}) collective-permute-start(f32[64,128]{1,0:T(8,128)S(1)} %get-tuple-element.10.own_ref), channel_id=1, source_target_pairs={{0,4},{1,5},{2,6},{3,7},{4,0},{5,1},{6,2},{7,3},{8,12},{9,13},{10,... | collective-permute-start | bytes 98312 | tf_op jit(solution)/shard_map/ppermute | solution.py:555
  34.2 0.0 copy-done
  34.2 0.0 copy-done.1
  34.2 3.1 %local_modes.1.kept_ref = f32[2,6,32,128]{3,2,1,0:T(8,128)S(1)} custom-call(bf16[2176,384]{1,0:T(8,128)(2,1)S(1)} %get-tuple-element.11.high_ref, bf16[2176,384]{1,0:T(8,128)(2,1)} %get-tuple-element.12.low_hbm, f32[6,128]{1,0:T(8,128)S(1)} %bitcast.7, f32[2,128,128]{2,1,0:T(8,128)S(1)} %copy-done.1, f32[32,128]{1,0:T(8,128)S(1)} %get-tuple-element.13.resp_ref), custom_call_target="tpu_custom_call" | custom-call | flops 3000000000 | bytes 8000000 | tf_op jit(solution)/shard_map/local_modes/pallas_call | solution.py:510
  37.3 0.6 %collective-permute-start.5 = (f32[6,32,128]{2,1,0:T(8,128)S(1)}, f32[6,32,128]{2,1,0:T(8,128)S(1)}, u32[]{:S(2)}, u32[]{:S(2)}) collective-permute-start(f32[6,32,128]{2,1,0:T(8,128)S(1)} %slice_bitcast_fusion), channel_id=1, source_target_pairs={{0,1},{1,0},{2,3},{3,2},{4,5},{5,4},{6,7},{7,6},{8,9},{9,8},{10,11... | collective-permute-start | bytes 294920 | tf_op jit(solution)/shard_map/ppermute | solution.py:555
  38.0 0.0 collective-permute-done.3.got_ref
  38.0 0.1 collective-permute-start.4
  38.0 1.2 %collective-permute-done.4.refs_1_ = f32[128,128]{1,0:T(8,128)S(1)} collective-permute-done((f32[128,128]{1,0:T(8,128)S(1)}, f32[128,128]{1,0:T(8,128)S(1)}, u32[]{:S(2)}, u32[]{:S(2)}) %collective-permute-start.4) | collective-permute-done | bytes 65568 | tf_op jit(solution)/shard_map/ppermute | solution.py:555
  39.3 1.7 %unpack_gram.1 = f32[32,2,32,32]{3,2,1,0:T(8,128)} custom-call(f32[128,128]{1,0:T(8,128)S(1)} %join_y.1.refs_0_, f32[128,128]{1,0:T(8,128)S(1)} %collective-permute-done.4.refs_1_), custom_call_target="tpu_custom_call" | custom-call | tf_op jit(solution)/shard_map/unpack_gram/pallas_call | solution.py:352
  41.0 1.0 %collective-permute-done.5.got_ref = f32[6,32,128]{2,1,0:T(8,128)S(1)} collective-permute-done((f32[6,32,128]{2,1,0:T(8,128)S(1)}, f32[6,32,128]{2,1,0:T(8,128)S(1)}, u32[]{:S(2)}, u32[]{:S(2)}) %collective-permute-start.5) | collective-permute-done | bytes 98336 | tf_op jit(solution)/shard_map/ppermute | solution.py:555
  42.0 0.8 %join_modes.1 = f32[32,2,768]{2,1,0:T(2,128)} custom-call(f32[2,6,32,128]{3,2,1,0:T(8,128)S(1)} %local_modes.1.kept_ref, f32[6,32,128]{2,1,0:T(8,128)S(1)} %collective-permute-done.5.got_ref), custom_call_target="tpu_custom_call" | custom-call | tf_op jit(solution)/shard_map/join_modes/pallas_call | solution.py:352
  (5 shorter events, 0.1 us)
Async XLA Ops:
  1.4 32.8 %copy-start = (f32[768]{0:T(1024)S(1)}, f32[768]{0:T(1024)}, u32[]{:S(2)}) copy-start(f32[768]{0:T(1024)} %param.5) | copy-start | bytes 9220
  1.4 32.8 %copy-start.1 = (f32[2,128,128]{2,1,0:T(8,128)S(1)}, f32[2,128,128]{2,1,0:T(8,128)}, u32[]{:S(2)}) copy-start(f32[2,128,128]{2,1,0:T(8,128)} %constant.5.clone.table_ref) | copy-start | bytes 393220
  12.0 1.5 %collective-permute-start = (f32[288,128]{1,0:T(8,128)S(1)}, f32[288,128]{1,0:T(8,128)S(1)}, u32[]{:S(2)}, u32[]{:S(2)}) collective-permute-start(f32[288,128]{1,0:T(8,128)S(1)} %get-tuple-element.9), channel_id=1, source_target_pairs={{0,2},{1,3},{2,0},{3,1},{4,6},{5,7},{6,4},{7,5},{8,10},{9,11},{10,... | collective-permute-start | bytes 442376 | tf_op jit(solution)/shard_map/ppermute | solution.py:555
  24.0 4.2 %collective-permute-start.1 = (f32[96,128]{1,0:T(8,128)S(1)}, f32[96,128]{1,0:T(8,128)S(1)}, u32[]{:S(2)}, u32[]{:S(2)}) collective-permute-start(f32[96,128]{1,0:T(8,128)S(1)} %add_near.1.kept_ref), channel_id=1, source_target_pairs={{0,8},{1,9},{2,10},{3,11},{4,12},{5,13},{6,14},{7,15},{8,0},{9,1},... | collective-permute-start | bytes 147464 | tf_op jit(solution)/shard_map/ppermute | solution.py:555
  28.2 5.0 %collective-permute-start.2 = (f32[96,128]{1,0:T(8,128)S(1)}, f32[96,128]{1,0:T(8,128)S(1)}, u32[]{:S(2)}, u32[]{:S(2)}) collective-permute-start(f32[96,128]{1,0:T(8,128)S(1)} %add_z.1.kept_ref), channel_id=1, source_target_pairs={{0,16},{1,17},{2,18},{3,19},{4,20},{5,21},{6,22},{7,23},{8,24},{9,... | collective-permute-start | bytes 147464 | tf_op jit(solution)/shard_map/ppermute | solution.py:555
  33.4 4.6 %collective-permute-start.3 = (f32[64,128]{1,0:T(8,128)S(1)}, f32[64,128]{1,0:T(8,128)S(1)}, u32[]{:S(2)}, u32[]{:S(2)}) collective-permute-start(f32[64,128]{1,0:T(8,128)S(1)} %get-tuple-element.10.own_ref), channel_id=1, source_target_pairs={{0,4},{1,5},{2,6},{3,7},{4,0},{5,1},{6,2},{7,3},{8,12},{9,13},{10,... | collective-permute-start | bytes 98312 | tf_op jit(solution)/shard_map/ppermute | solution.py:555
  37.3 4.7 %collective-permute-start.5 = (f32[6,32,128]{2,1,0:T(8,128)S(1)}, f32[6,32,128]{2,1,0:T(8,128)S(1)}, u32[]{:S(2)}, u32[]{:S(2)}) collective-permute-start(f32[6,32,128]{2,1,0:T(8,128)S(1)} %slice_bitcast_fusion), channel_id=1, source_target_pairs={{0,1},{1,0},{2,3},{3,2},{4,5},{5,4},{6,7},{7,6},{8,9},{9,8},{10,11... | collective-permute-start | bytes 294920 | tf_op jit(solution)/shard_map/ppermute | solution.py:555
  38.0 1.3 %collective-permute-start.4 = (f32[128,128]{1,0:T(8,128)S(1)}, f32[128,128]{1,0:T(8,128)S(1)}, u32[]{:S(2)}, u32[]{:S(2)}) collective-permute-start(f32[128,128]{1,0:T(8,128)S(1)} %join_y.1.refs_0_), channel_id=1, source_target_pairs={{0,2},{1,3},{2,0},{3,1},{4,6},{5,7},{6,4},{7,5},{8,10},{9,11},{10,... | collective-permute-start | bytes 196616 | tf_op jit(solution)/shard_map/ppermute | solution.py:555
where the time goes:
time: 43.1 us; the launch traced here: 42.8 us
  Pallas kernels  16.4 us (38%)
  blocking collectives  10.4 us (24%)
  waiting for transfers between devices  8.21 us (19%)
  starting transfers between devices  6.29 us (15%)
  other arithmetic  0.77 us (2%)
  between operations  0.7 us (2%)
    pallas_call x1, Pallas kernels, gram_parts(): pl.pallas_call(functools.partial(gram_kernel, total_rows, places, by_core...  10.6 us
    all_to_all x1, blocking collectives, direction_shards(): lax.all_to_all(parts, ('pts', 'freq'), 0, 0, axis_index_groups=near, tile...  10.4 us
    ppermute x6, waiting for transfers between devices, swap(): lax.ppermute(value, ('pts', 'freq'), [(i, i ^ mask) for i in range(n_devi...  8.21 us
    ppermute x6, starting transfers between devices, swap(): lax.ppermute(value, ('pts', 'freq'), [(i, i ^ mask) for i in range(n_devi...  6.29 us
    pallas_call x1, Pallas kernels, local_modes(): pl.pallas_call(functools.partial(modes_kernel, total_rows), out_shape=flo...  3.14 us
    pallas_call x7, Pallas kernels, call(): pl.pallas_call(kernel, out_shape=out_shape, in_specs=[VMEM] * len(args),...  2.65 us
  transfers between devices with their start and end apart: 6, of which 5 were waited for; matrix products, arithmetic and copies ran while one was open for 0% of the time, Pallas kernels for 11%

commit v1 on v0

--- a/solution.py
+++ b/solution.py
@@ -33,6 +33,11 @@
     high = table.astype(jnp.bfloat16)
     low = (table - high.astype(np.float64)).astype(jnp.bfloat16)
     return high, low
+
+
+def window_leaks():
+    real, _ = dft_values()
+    return [float(np.sum(real[k])) for k in range(2)]
 
 
 def mode_tables():
@@ -141,6 +146,7 @@
     keep_ref,
     send_ref,
     high_ref,
+    rest_ref,
     low_hbm,
     x_ref,
     dft_ref,
@@ -156,62 +162,87 @@
     out_sem,
 ):
     times, cols = x_ref.shape
-    halves = times // HALF
     col_tiles = cols // LANES
-    pieces = in_sems.shape[0]
-    piece = times // pieces
+    pieces = NB // 2
+    tail = times - pieces * NFFT
+
+    def piece_rows(i):
+        return pl.ds(i * NFFT, NFFT) if isinstance(i, int) else pl.ds(pl.multiple_of(i * NFFT, NFFT), NFFT)
 
     def fetch(i):
-        rows = pl.ds(i * piece, piece)
+        rows = piece_rows(i)
         return pltpu.make_async_copy(x_hbm.at[rows], x_ref.at[rows], in_sems.at[i])
 
+    tail_rows = pl.ds(pieces * NFFT, tail)
+    fetch_tail = pltpu.make_async_copy(x_hbm.at[tail_rows], x_ref.at[tail_rows], in_sems.at[pieces])
     for i in range(pieces):
         fetch(i).start()
+    fetch_tail.start()
     fill_dft(dft_ref)
     spread_start(aux_ref, spread_ref)
-
-    acc = jnp.zeros((HALF, cols), jnp.float32)
-    for i in range(pieces):
-        fetch(i).wait()
-        for h in range(piece // HALF):
-            acc = acc + x_ref[pl.ds(i * piece + h * HALF, HALF), :]
-    mean = jnp.sum(acc, axis=0, keepdims=True) / times
     weights = load_weights(aux_ref.at[pl.ds(2 * NB, aux_ref.shape[0] - 2 * NB)], col_tiles)
     scale = jnp.sqrt(weights / (2.0 * total_rows))
-
-    def center(i, carry):
-        rows = pl.ds(pl.multiple_of(i * HALF, HALF), HALF)
-        high, low = split((x_ref[rows, :] - mean) * scale)
+    fetch(0).wait()
+    first_mean = jnp.mean(x_ref[pl.ds(0, NFFT), :], axis=0, keepdims=True)
+
+    def center(rows, acc):
+        value = x_ref[rows, :] - first_mean
+        high, low = split(value * scale)
         high_ref[rows, :] = high
         low_ref[rows, :] = low
-        return carry
-
-    lax.fori_loop(0, halves, center, 0, unroll=3)
+        for h in range(value.shape[0] // HALF):
+            acc = acc + value[h * HALF : (h + 1) * HALF]
+        return acc
+
+    def transform(i):
+        blocks = []
+        for s in range(2):
+            start = (2 * i + s) * HALF
+            rows = pl.ds(start if isinstance(i, int) else pl.multiple_of(start, HALF), NFFT)
+            blocks.append(jnp.concatenate([high_ref[rows, :], low_ref[rows, :]], axis=0))
+        both = jnp.dot(
+            dft_ref[...], jnp.concatenate(blocks, axis=1), preferred_element_type=jnp.float32
+        )
+        return both[: 2 * NF] + both[2 * NF :]
+
+    def store(i, spectrum):
+        for s in range(2):
+            for o in range(2 * NF // 8):
+                for c in range(col_tiles):
+                    first = s * cols + c * LANES
+                    rows = pl.ds(ROW_STEP * (2 * i + s), 8, stride=FREQ_STEP)
+                    spec_ref[c, o, rows, :] = spectrum[8 * o : 8 * o + 8, first : first + LANES]
+
+    acc = center(piece_rows(0), jnp.zeros((HALF, cols), jnp.float32))
+    fetch(1).wait()
+    acc = center(piece_rows(1), acc)
+
+    def stream(i, acc):
+        fetch(i + 2).wait()
+        spectrum = transform(i)
+        acc = center(piece_rows(i + 2), acc)
+        store(i, spectrum)
+        return acc
+
+    acc = lax.fori_loop(0, pieces - 2, stream, acc, unroll=2)
+    fetch_tail.wait()
+    spectrum = transform(pieces - 2)
+    acc = center(tail_rows, acc)
+    store(pieces - 2, spectrum)
+    store(pieces - 1, transform(pieces - 1))
     pad = high_ref.shape[0] - times
     if pad:
         high_ref[pl.ds(times, pad), :] = jnp.zeros((pad, cols), jnp.bfloat16)
         low_ref[pl.ds(times, pad), :] = jnp.zeros((pad, cols), jnp.bfloat16)
     save_low = pltpu.make_async_copy(low_ref, low_hbm, out_sem)
     save_low.start()
-
-    def transform(i, carry):
-        blocks = []
-        for s in range(2):
-            rows = pl.ds(pl.multiple_of((2 * i + s) * HALF, HALF), NFFT)
-            blocks.append(jnp.concatenate([high_ref[rows, :], low_ref[rows, :]], axis=0))
-        both = jnp.dot(
-            dft_ref[...], jnp.concatenate(blocks, axis=1), preferred_element_type=jnp.float32
-        )
-        spectrum = both[: 2 * NF] + both[2 * NF :]
-        for s in range(2):
-            for o in range(2 * NF // 8):
-                for c in range(col_tiles):
-                    first = s * cols + c * LANES
-                    rows = pl.ds(ROW_STEP * (2 * i + s), 8, stride=FREQ_STEP)
-                    spec_ref[c, o, rows, :] = spectrum[8 * o : 8 * o + 8, first : first + LANES]
-        return carry
-
-    lax.fori_loop(0, NB // 2, transform, 0, unroll=2)
+    rest = jnp.sum(acc, axis=0, keepdims=True) / times * scale
+    rest_ref[...] = jnp.broadcast_to(rest, rest_ref.shape)
+    for k, leak in enumerate(window_leaks()):
+        rows = pl.ds(FREQ_STEP * k, NB, stride=ROW_STEP)
+        for c in range(col_tiles):
+            part = rest[:, c * LANES : (c + 1) * LANES]
+            spec_ref[c, 0, rows, :] = spec_ref[c, 0, rows, :] - leak * part
 
     row = lax.broadcasted_iota(jnp.int32, (NB, LANES), 0)
     lane = lax.broadcasted_iota(jnp.int32, (NB, LANES), 1)
@@ -297,15 +328,14 @@
     start = jnp.transpose(start_vec, (1, 2, 0)).reshape(2 * NB, NF)
     start = jnp.pad(start, ((0, 0), (0, LANES - NF)))
     aux = jnp.concatenate([start, weight_rows], axis=0)
-    pieces = 11
     any_space = pl.BlockSpec(memory_space=pl.ANY)
     saved = jax.ShapeDtypeStruct((-(-times // LANES) * LANES, cols), jnp.bfloat16)
     half = floats(NF // 4 * NB // 2 + RESP_ROWS, LANES)
     return pl.pallas_call(
         functools.partial(gram_kernel, total_rows, places, by_core),
-        out_shape=(half, half, saved, saved),
+        out_shape=(half, half, saved, floats(8, cols), saved),
         in_specs=[any_space, VMEM],
-        out_specs=(VMEM, VMEM, VMEM, any_space),
+        out_specs=(VMEM, VMEM, VMEM, VMEM, any_space),
         scratch_shapes=[
             pltpu.VMEM((times, cols), jnp.float32),
             pltpu.VMEM((4 * NF, 2 * NFFT), jnp.bfloat16),
@@ -317,7 +347,7 @@
             pltpu.VMEM((NF // PACK, NB, LANES), jnp.float32),
             pltpu.VMEM((NF // PACK, 2 * NB, LANES), jnp.float32),
             pltpu.VMEM((NF // 2 * NB // 2 + RESP_ROWS, LANES), jnp.float32),
-            pltpu.SemaphoreType.DMA((pieces,)),
+            pltpu.SemaphoreType.DMA((NB // 2 + 1,)),
             pltpu.SemaphoreType.DMA(()),
         ],
         compiler_params=pltpu.CompilerParams(vmem_limit_bytes=VMEM_LIMIT),
@@ -448,11 +478,21 @@
 
 
 def modes_kernel(
-    total_rows, high_ref, low_hbm, w_ref, table_ref, resp_ref, out_ref, low_ref, a_ref, sem
+    total_rows, high_ref, low_hbm, rest_ref, w_ref, table_ref, resp_ref, out_ref, low_ref, a_ref, sems
 ):
     padded, cols = high_ref.shape
-    fetch_low = pltpu.make_async_copy(low_hbm, low_ref, sem)
-    fetch_low.start()
+    pieces = sems.shape[0]
+    fetches = []
+    for i in range(pieces):
+        first = padded // LANES * i // pieces * LANES
+        last = padded // LANES * (i + 1) // pieces * LANES
+        rows = pl.ds(first, last - first)
+        fetches.append(pltpu.make_async_copy(low_hbm.at[rows], low_ref.at[rows], sems.at[i]))
+    for fetch in fetches:
+        fetch.start()
+    row = lax.broadcasted_iota(jnp.int32, (RESP_ROWS, 1), 0)
+    leaks = window_leaks()
+    corrections = []
     groups = RESP_ROWS // 2
     lane = lax.broadcasted_iota(jnp.int32, (RESP_ROWS, LANES), 1)
     left = lane < HALF
@@ -460,6 +500,11 @@
         resp = resp_ref[...]
         if q:
             resp = pltpu.roll(resp, LANES - q * NB, 1)
+        if q < len(leaks):
+            total = jnp.sum(jnp.where(lane < NB, resp, 0.0), axis=1, keepdims=True) * leaks[q]
+            corrections.append(jnp.where(row % groups == 0, total, 0.0) * rest_ref[pl.ds(0, 1), :])
+        else:
+            corrections.append(jnp.zeros((RESP_ROWS, cols), jnp.float32))
         real = jnp.concatenate([resp[:groups]] * 2, axis=0)
         imag = jnp.concatenate([resp[groups:]] * 2, axis=0)
         rows = pl.ds(q * RESP_ROWS, RESP_ROWS)
@@ -486,7 +531,9 @@
             a_ref[pl.ds(2 * NF + q * RESP_ROWS, RESP_ROWS), own] = low
     both = jnp.dot(a_ref[...], high_ref[...], preferred_element_type=jnp.float32)
     modes = both[: 2 * NF] + both[2 * NF :]
-    fetch_low.wait()
+    modes -= jnp.concatenate(corrections, axis=0)
+    for fetch in fetches:
+        fetch.wait()
     modes += jnp.dot(
         a_ref[pl.ds(0, 2 * NF), :], low_ref[...], preferred_element_type=jnp.float32
     )
@@ -505,24 +552,24 @@
                     ]
 
 
-def local_modes(high, low, weight_rows, response, total_rows, n_freq):
+def local_modes(high, low, rest, weight_rows, response, total_rows, n_freq):
     padded, cols = high.shape
     return pl.pallas_call(
         functools.partial(modes_kernel, total_rows),
         out_shape=floats(n_freq, 2 * cols // LANES, NF // n_freq, LANES),
-        in_specs=[VMEM, pl.BlockSpec(memory_space=pl.ANY)] + [VMEM] * 3,
+        in_specs=[VMEM, pl.BlockSpec(memory_space=pl.ANY)] + [VMEM] * 4,
         out_specs=VMEM,
         scratch_shapes=[
             pltpu.VMEM((padded, cols), jnp.bfloat16),
             pltpu.VMEM((4 * NF, padded), jnp.bfloat16),
-            pltpu.SemaphoreType.DMA(()),
+            pltpu.SemaphoreType.DMA((4,)),
         ],
         compiler_params=pltpu.CompilerParams(vmem_limit_bytes=VMEM_LIMIT),
         cost_estimate=pl.CostEstimate(
             flops=3_000_000_000, bytes_accessed=8_000_000, transcendentals=0
         ),
         name="local_modes",
-    )(high, low, weight_rows, jnp.asarray(mode_tables()), response)
+    )(high, low, rest, weight_rows, jnp.asarray(mode_tables()), response)
 
 
 def join_kernel(kept_ref, got_ref, out_ref):
@@ -565,7 +612,7 @@
     places = [
         (i // 8 % 2) * 16 + (i // 4 % 2) * 8 + (i // 16) * 4 + i % 4 for i in range(NF // 2)
     ]
-    keep, send, high, low = gram_parts(
+    keep, send, high, rest, low = gram_parts(
         snapshots, weight_rows, start_vec, total_rows, places, True
     )
     parts = add_core(keep, swap(send, core))
@@ -576,7 +623,7 @@
     part = add("add_z", part, swap(part, z_near))
     packed, response = finish(part, swap(part, z_far))
     other = swap(packed, y)
-    modes = local_modes(high, low, weight_rows, response, total_rows, 2)
+    modes = local_modes(high, low, rest, weight_rows, response, total_rows, 2)
     packed = small_call(join_y_kernel, "join_y", floats(2 * packed.shape[0], LANES))(packed, other)
     gram_mine = unpack_gram(packed, swap(packed, core))
     return gram_mine, join_modes(modes, swap(modes[1], x))
@@ -590,7 +637,7 @@
     group = lax.axis_index("freq")
     weight_rows = weight.reshape(-1, LANES)
     places = list(range(NF // 2))
-    first, second, high, low = gram_parts(
+    first, second, high, rest, low = gram_parts(
         snapshots, weight_rows, start_vec, total_rows, places, False
     )
     parts = jnp.concatenate([first[:-RESP_ROWS], second[:-RESP_ROWS]], axis=0)
@@ -602,7 +649,7 @@
     response = lax.all_gather(response_of(gram_mine, start_mine), "freq", axis=0, tiled=True)
     response = jnp.transpose(response.reshape(NF // PACK, PACK, 2, NB), (2, 0, 1, 3))
     response = response.reshape(RESP_ROWS, LANES)
-    modes = local_modes(high, low, weight_rows, response, total_rows, n_freq)
+    modes = local_modes(high, low, rest, weight_rows, response, total_rows, n_freq)
     modes = lax.all_to_all(modes, "freq", 0, 0, tiled=True)
     modes = modes.reshape(n_freq, cols // LANES, 2, mine_count, LANES)
     modes = jnp.transpose(modes, (3, 2, 0, 1, 4)).reshape(mine_count, 2, n_freq * cols)

time: 43.1 us -> 43.7 us (1.014)
  Pallas kernels: 16.4 us -> 17 us
    pallas_call x1, Pallas kernels: 10.6 us -> 11.3 us  [gram_parts(): pl.pallas_call(functools.partial(gram_kernel, total_rows, places, by_core...]
where the time goes in v1:
time: 43.7 us; the launch traced here: 43.4 us
  Pallas kernels  17 us (39%)
  blocking collectives  10.4 us (24%)
  waiting for transfers between devices  8.18 us (19%)
  starting transfers between devices  6.33 us (14%)
  other arithmetic  0.77 us (2%)
  between operations  0.7 us (2%)
    pallas_call x1, Pallas kernels, gram_parts(): pl.pallas_call(functools.partial(gram_kernel, total_rows, places, by_core...  11.3 us
    all_to_all x1, blocking collectives, direction_shards(): lax.all_to_all(parts, ('pts', 'freq'), 0, 0, axis_index_groups=near, tile...  10.4 us
    ppermute x6, waiting for transfers between devices, swap(): lax.ppermute(value, ('pts', 'freq'), [(i, i ^ mask) for i in range(n_devi...  8.18 us
    ppermute x6, starting transfers between devices, swap(): lax.ppermute(value, ('pts', 'freq'), [(i, i ^ mask) for i in range(n_devi...  6.33 us
    pallas_call x1, Pallas kernels, local_modes(): pl.pallas_call(functools.partial(modes_kernel, total_rows), out_shape=flo...  3.13 us
    pallas_call x7, Pallas kernels, call(): pl.pallas_call(kernel, out_shape=out_shape, in_specs=[VMEM] * len(args),...  2.65 us
  transfers between devices with their start and end apart: 6, of which 5 were waited for; matrix products, arithmetic and copies ran while one was open for 0% of the time, Pallas kernels for 11%

profile of v1, /device:TPU:0, one launch (start us, length us, event | category | flops | bytes accessed | tf_op | source)
XLA Modules:
  0.0 43.4 jit_solution(10028892677765191521)
XLA Ops:
  0.6 0.8 %select_maximum_fusion.aux_ref = f32[70,128]{1,0:T(8,128)S(1)} fusion(f32[64,64]{1,0:T(8,128)} %bitcast.8, f32[6,128]{1,0:T(8,128)} %bitcast.6), kind=kLoop, calls=%fused_computation.1 | loop fusion | flops 26880 | bytes 55296 | tf_op jit(solution)/shard_map/concatenate | solution.py:330
  1.4 0.0 copy-start
  1.4 0.0 copy-start.1
  1.4 11.3 %gram_parts.1 = (f32[288,128]{1,0:T(8,128)S(1)}, f32[288,128]{1,0:T(8,128)S(1)}, bf16[2176,384]{1,0:T(8,128)(2,1)S(1)}, f32[8,384]{1,0:T(8,128)S(1)}, bf16[2176,384]{1,0:T(8,128)(2,1)}) custom-call(f32[2112,384]{1,0:T(8,128)} %x_hbm.1, f32[70,128]{1,0:T(8,128)S(1)} %select_maximum_fusion.aux_ref), custom_call_target="tpu_custom_call" | custom-call | flops 5000000000 | bytes 8000000 | tf_op jit(solution)/shard_map/gram_parts/pallas_call | solution.py:334
  12.7 0.5 %collective-permute-start = (f32[288,128]{1,0:T(8,128)S(1)}, f32[288,128]{1,0:T(8,128)S(1)}, u32[]{:S(2)}, u32[]{:S(2)}) collective-permute-start(f32[288,128]{1,0:T(8,128)S(1)} %get-tuple-element.10), channel_id=1, source_target_pairs={{0,2},{1,3},{2,0},{3,1},{4,6},{5,7},{6,4},{7,5},{8,10},{9,11},{10,... | collective-permute-start | bytes 442376 | tf_op jit(solution)/shard_map/ppermute | solution.py:602
  13.2 1.0 %collective-permute-done.got_ref = f32[288,128]{1,0:T(8,128)S(1)} collective-permute-done((f32[288,128]{1,0:T(8,128)S(1)}, f32[288,128]{1,0:T(8,128)S(1)}, u32[]{:S(2)}, u32[]{:S(2)}) %collective-permute-start) | collective-permute-done | bytes 147488 | tf_op jit(solution)/shard_map/ppermute | solution.py:602
  14.2 10.4 %all_to_all.5.parts_ref = f32[4,96,128]{2,1,0:T(8,128)S(1)} all-to-all(f32[4,96,128]{2,1,0:T(8,128)S(1)} %add_core.1), channel_id=1, replica_groups={{0,1,4,5},{2,3,6,7},{8,9,12,13},{10,11,14,15},{16,17,20,21},{18,19,22,2..., dimensions={0} | all-to-all | bytes 393216 | tf_op jit(solution)/shard_map/all_to_all | solution.py:619
  24.7 1.6 %collective-permute-start.1 = (f32[96,128]{1,0:T(8,128)S(1)}, f32[96,128]{1,0:T(8,128)S(1)}, u32[]{:S(2)}, u32[]{:S(2)}) collective-permute-start(f32[96,128]{1,0:T(8,128)S(1)} %add_near.1.kept_ref), channel_id=1, source_target_pairs={{0,8},{1,9},{2,10},{3,11},{4,12},{5,13},{6,14},{7,15},{8,0},{9,1},... | collective-permute-start | bytes 147464 | tf_op jit(solution)/shard_map/ppermute | solution.py:602
  26.3 2.5 %collective-permute-done.1.got_ref = f32[96,128]{1,0:T(8,128)S(1)} collective-permute-done((f32[96,128]{1,0:T(8,128)S(1)}, f32[96,128]{1,0:T(8,128)S(1)}, u32[]{:S(2)}, u32[]{:S(2)}) %collective-permute-start.1) | collective-permute-done | bytes 49184 | tf_op jit(solution)/shard_map/ppermute | solution.py:602
  28.8 2.7 %collective-permute-start.2 = (f32[96,128]{1,0:T(8,128)S(1)}, f32[96,128]{1,0:T(8,128)S(1)}, u32[]{:S(2)}, u32[]{:S(2)}) collective-permute-start(f32[96,128]{1,0:T(8,128)S(1)} %add_z.1.kept_ref), channel_id=1, source_target_pairs={{0,16},{1,17},{2,18},{3,19},{4,20},{5,21},{6,22},{7,23},{8,24},{9,... | collective-permute-start | bytes 147464 | tf_op jit(solution)/shard_map/ppermute | solution.py:602
  31.5 2.4 %collective-permute-done.2.got_ref = f32[96,128]{1,0:T(8,128)S(1)} collective-permute-done((f32[96,128]{1,0:T(8,128)S(1)}, f32[96,128]{1,0:T(8,128)S(1)}, u32[]{:S(2)}, u32[]{:S(2)}) %collective-permute-start.2) | collective-permute-done | bytes 49184 | tf_op jit(solution)/shard_map/ppermute | solution.py:602
  33.9 0.1 finish.1
  34.0 0.8 %collective-permute-start.3 = (f32[64,128]{1,0:T(8,128)S(1)}, f32[64,128]{1,0:T(8,128)S(1)}, u32[]{:S(2)}, u32[]{:S(2)}) collective-permute-start(f32[64,128]{1,0:T(8,128)S(1)} %get-tuple-element.11.own_ref), channel_id=1, source_target_pairs={{0,4},{1,5},{2,6},{3,7},{4,0},{5,1},{6,2},{7,3},{8,12},{9,13},{10,... | collective-permute-start | bytes 98312 | tf_op jit(solution)/shard_map/ppermute | solution.py:602
  34.8 0.0 copy-done
  34.8 0.0 copy-done.1
  34.8 3.1 %local_modes.1.kept_ref = f32[2,6,32,128]{3,2,1,0:T(8,128)S(1)} custom-call(bf16[2176,384]{1,0:T(8,128)(2,1)S(1)} %get-tuple-element.12.high_ref, bf16[2176,384]{1,0:T(8,128)(2,1)} %get-tuple-element.13.low_hbm, f32[8,384]{1,0:T(8,128)S(1)} %get-tuple-element.14.rest_ref, f32[6,128]{1,0:T(8,128)S(1)} %bitcast.7, f32[2,128,128]{2,1,0:T(8,128)S(1)} %copy-done.1, ...), custom_call_target="tpu_custom_call" | custom-call | flops 3000000000 | bytes 8000000 | tf_op jit(solution)/shard_map/local_modes/pallas_call | solution.py:557
  37.9 0.6 %collective-permute-start.5 = (f32[6,32,128]{2,1,0:T(8,128)S(1)}, f32[6,32,128]{2,1,0:T(8,128)S(1)}, u32[]{:S(2)}, u32[]{:S(2)}) collective-permute-start(f32[6,32,128]{2,1,0:T(8,128)S(1)} %slice_bitcast_fusion), channel_id=1, source_target_pairs={{0,1},{1,0},{2,3},{3,2},{4,5},{5,4},{6,7},{7,6},{8,9},{9,8},{10,11... | collective-permute-start | bytes 294920 | tf_op jit(solution)/shard_map/ppermute | solution.py:602
  38.6 0.0 collective-permute-done.3.got_ref
  38.6 0.1 collective-permute-start.4
  38.7 1.2 %collective-permute-done.4.refs_1_ = f32[128,128]{1,0:T(8,128)S(1)} collective-permute-done((f32[128,128]{1,0:T(8,128)S(1)}, f32[128,128]{1,0:T(8,128)S(1)}, u32[]{:S(2)}, u32[]{:S(2)}) %collective-permute-start.4) | collective-permute-done | bytes 65568 | tf_op jit(solution)/shard_map/ppermute | solution.py:602
  39.9 1.7 %unpack_gram.1 = f32[32,2,32,32]{3,2,1,0:T(8,128)} custom-call(f32[128,128]{1,0:T(8,128)S(1)} %join_y.1.refs_0_, f32[128,128]{1,0:T(8,128)S(1)} %collective-permute-done.4.refs_1_), custom_call_target="tpu_custom_call" | custom-call | tf_op jit(solution)/shard_map/unpack_gram/pallas_call | solution.py:382
  41.6 1.0 %collective-permute-done.5.got_ref = f32[6,32,128]{2,1,0:T(8,128)S(1)} collective-permute-done((f32[6,32,128]{2,1,0:T(8,128)S(1)}, f32[6,32,128]{2,1,0:T(8,128)S(1)}, u32[]{:S(2)}, u32[]{:S(2)}) %collective-permute-start.5) | collective-permute-done | bytes 98336 | tf_op jit(solution)/shard_map/ppermute | solution.py:602
  42.6 0.8 %join_modes.1 = f32[32,2,768]{2,1,0:T(2,128)} custom-call(f32[2,6,32,128]{3,2,1,0:T(8,128)S(1)} %local_modes.1.kept_ref, f32[6,32,128]{2,1,0:T(8,128)S(1)} %collective-permute-done.5.got_ref), custom_call_target="tpu_custom_call" | custom-call | tf_op jit(solution)/shard_map/join_modes/pallas_call | solution.py:382
  (5 shorter events, 0.1 us)
Async XLA Ops:
  1.4 33.4 %copy-start = (f32[768]{0:T(1024)S(1)}, f32[768]{0:T(1024)}, u32[]{:S(2)}) copy-start(f32[768]{0:T(1024)} %param.5) | copy-start | bytes 9220
  1.4 33.4 %copy-start.1 = (f32[2,128,128]{2,1,0:T(8,128)S(1)}, f32[2,128,128]{2,1,0:T(8,128)}, u32[]{:S(2)}) copy-start(f32[2,128,128]{2,1,0:T(8,128)} %constant.5.clone.table_ref) | copy-start | bytes 393220
  12.7 1.5 %collective-permute-start = (f32[288,128]{1,0:T(8,128)S(1)}, f32[288,128]{1,0:T(8,128)S(1)}, u32[]{:S(2)}, u32[]{:S(2)}) collective-permute-start(f32[288,128]{1,0:T(8,128)S(1)} %get-tuple-element.10), channel_id=1, source_target_pairs={{0,2},{1,3},{2,0},{3,1},{4,6},{5,7},{6,4},{7,5},{8,10},{9,11},{10,... | collective-permute-start | bytes 442376 | tf_op jit(solution)/shard_map/ppermute | solution.py:602
  24.7 4.2 %collective-permute-start.1 = (f32[96,128]{1,0:T(8,128)S(1)}, f32[96,128]{1,0:T(8,128)S(1)}, u32[]{:S(2)}, u32[]{:S(2)}) collective-permute-start(f32[96,128]{1,0:T(8,128)S(1)} %add_near.1.kept_ref), channel_id=1, source_target_pairs={{0,8},{1,9},{2,10},{3,11},{4,12},{5,13},{6,14},{7,15},{8,0},{9,1},... | collective-permute-start | bytes 147464 | tf_op jit(solution)/shard_map/ppermute | solution.py:602
  28.8 5.0 %collective-permute-start.2 = (f32[96,128]{1,0:T(8,128)S(1)}, f32[96,128]{1,0:T(8,128)S(1)}, u32[]{:S(2)}, u32[]{:S(2)}) collective-permute-start(f32[96,128]{1,0:T(8,128)S(1)} %add_z.1.kept_ref), channel_id=1, source_target_pairs={{0,16},{1,17},{2,18},{3,19},{4,20},{5,21},{6,22},{7,23},{8,24},{9,... | collective-permute-start | bytes 147464 | tf_op jit(solution)/shard_map/ppermute | solution.py:602
  34.0 4.6 %collective-permute-start.3 = (f32[64,128]{1,0:T(8,128)S(1)}, f32[64,128]{1,0:T(8,128)S(1)}, u32[]{:S(2)}, u32[]{:S(2)}) collective-permute-start(f32[64,128]{1,0:T(8,128)S(1)} %get-tuple-element.11.own_ref), channel_id=1, source_target_pairs={{0,4},{1,5},{2,6},{3,7},{4,0},{5,1},{6,2},{7,3},{8,12},{9,13},{10,... | collective-permute-start | bytes 98312 | tf_op jit(solution)/shard_map/ppermute | solution.py:602
  37.9 4.7 %collective-permute-start.5 = (f32[6,32,128]{2,1,0:T(8,128)S(1)}, f32[6,32,128]{2,1,0:T(8,128)S(1)}, u32[]{:S(2)}, u32[]{:S(2)}) collective-permute-start(f32[6,32,128]{2,1,0:T(8,128)S(1)} %slice_bitcast_fusion), channel_id=1, source_target_pairs={{0,1},{1,0},{2,3},{3,2},{4,5},{5,4},{6,7},{7,6},{8,9},{9,8},{10,11... | collective-permute-start | bytes 294920 | tf_op jit(solution)/shard_map/ppermute | solution.py:602
  38.6 1.3 %collective-permute-start.4 = (f32[128,128]{1,0:T(8,128)S(1)}, f32[128,128]{1,0:T(8,128)S(1)}, u32[]{:S(2)}, u32[]{:S(2)}) collective-permute-start(f32[128,128]{1,0:T(8,128)S(1)} %join_y.1.refs_0_), channel_id=1, source_target_pairs={{0,2},{1,3},{2,0},{3,1},{4,6},{5,7},{6,4},{7,5},{8,10},{9,11},{10,... | collective-permute-start | bytes 196616 | tf_op jit(solution)/shard_map/ppermute | solution.py:602

commit v2 on v0

--- a/solution.py
+++ b/solution.py
@@ -108,8 +108,23 @@
     return out
 
 
-ROW_STEP = 3
-FREQ_STEP = ROW_STEP * NB + 1
+TILE = 8
+
+
+def turn_tiles(tiles):
+    row = lax.broadcasted_iota(jnp.int32, (TILE, LANES), 0)
+    step = TILE // 2
+    while step:
+        keep = row % (2 * step) < step
+        turned = list(tiles)
+        for i in range(TILE):
+            if i % (2 * step) < step:
+                low, high = tiles[i], tiles[i + step]
+                turned[i] = jnp.where(keep, low, pltpu.roll(high, step, 0))
+                turned[i + step] = jnp.where(keep, pltpu.roll(low, TILE - step, 0), high)
+        tiles = turned
+        step //= 2
+    return tiles
 
 
 def core_bit():
@@ -145,6 +160,8 @@
     x_ref,
     dft_ref,
     low_ref,
+    block_even,
+    block_odd,
     spec_ref,
     z_even,
     z_odd,
@@ -158,6 +175,7 @@
     times, cols = x_ref.shape
     halves = times // HALF
     col_tiles = cols // LANES
+    block_refs = (block_even, block_odd)
     pieces = in_sems.shape[0]
     piece = times // pieces
 
@@ -194,24 +212,34 @@
     save_low = pltpu.make_async_copy(low_ref, low_hbm, out_sem)
     save_low.start()
 
-    def transform(i, carry):
-        blocks = []
-        for s in range(2):
-            rows = pl.ds(pl.multiple_of((2 * i + s) * HALF, HALF), NFFT)
-            blocks.append(jnp.concatenate([high_ref[rows, :], low_ref[rows, :]], axis=0))
-        both = jnp.dot(
-            dft_ref[...], jnp.concatenate(blocks, axis=1), preferred_element_type=jnp.float32
-        )
-        spectrum = both[: 2 * NF] + both[2 * NF :]
-        for s in range(2):
-            for o in range(2 * NF // 8):
-                for c in range(col_tiles):
-                    first = s * cols + c * LANES
-                    rows = pl.ds(ROW_STEP * (2 * i + s), 8, stride=FREQ_STEP)
-                    spec_ref[c, o, rows, :] = spectrum[8 * o : 8 * o + 8, first : first + LANES]
-        return carry
-
-    lax.fori_loop(0, NB // 2, transform, 0, unroll=2)
+    def transform(first):
+        for i in range(TILE // 2):
+            blocks = []
+            for s in range(2):
+                rows = pl.ds((first + 2 * i + s) * HALF, NFFT)
+                blocks.append(jnp.concatenate([high_ref[rows, :], low_ref[rows, :]], axis=0))
+            both = jnp.dot(
+                dft_ref[...], jnp.concatenate(blocks, axis=1), preferred_element_type=jnp.float32
+            )
+            spectrum = both[: 2 * NF] + both[2 * NF :]
+            for s in range(2):
+                block_refs[first // TILE % 2][2 * i + s] = spectrum[:, s * cols : (s + 1) * cols]
+
+    def arrange(first):
+        block_ref = block_refs[first // TILE % 2]
+        for c in range(col_tiles):
+            lanes = pl.ds(c * LANES, LANES)
+            for o in range(2 * NF // TILE):
+                rows = pl.ds(o * TILE, TILE)
+                tiles = turn_tiles([block_ref[b, rows, lanes] for b in range(TILE)])
+                for k in range(TILE):
+                    spec_ref[c, o * TILE + k, pl.ds(first, TILE), :] = tiles[k]
+
+    transform(0)
+    for first in range(0, NB, TILE):
+        if first + TILE < NB:
+            transform(first + TILE)
+        arrange(first)
 
     row = lax.broadcasted_iota(jnp.int32, (NB, LANES), 0)
     lane = lax.broadcasted_iota(jnp.int32, (NB, LANES), 1)
@@ -221,10 +249,9 @@
     def prepare(z_ref, octet, half):
         for part in range(2):
             for q in range(PACK):
-                rows = pl.ds(FREQ_STEP * (PACK * half + q), NB, stride=ROW_STEP)
                 own = pl.ds(part * LANES + q * NB, NB)
                 for c in range(col_tiles):
-                    value = spec_ref[c, octet + octets * part, rows, :]
+                    value = spec_ref[c, NF * part + TILE * octet + PACK * half + q]
                     high = value.astype(jnp.bfloat16)
                     low = (2.0 * (value - high.astype(jnp.float32))).astype(jnp.bfloat16)
                     z_ref[own, pl.ds(c * LANES, LANES)] = high
@@ -310,7 +337,9 @@
             pltpu.VMEM((times, cols), jnp.float32),
             pltpu.VMEM((4 * NF, 2 * NFFT), jnp.bfloat16),
             pltpu.VMEM(saved.shape, jnp.bfloat16),
-            pltpu.VMEM((cols // LANES, 2 * NF // 8, 8 * FREQ_STEP, LANES), jnp.float32),
+            pltpu.VMEM((TILE, 2 * NF, cols), jnp.float32),
+            pltpu.VMEM((TILE, 2 * NF, cols), jnp.float32),
+            pltpu.VMEM((cols // LANES, 2 * NF, NB, LANES), jnp.float32),
             pltpu.VMEM((2 * LANES, 2 * cols), jnp.bfloat16),
             pltpu.VMEM((2 * LANES, 2 * cols), jnp.bfloat16),
             pltpu.VMEM((NF // PACK, NB, LANES), jnp.float32),
@@ -448,11 +477,18 @@
 
 
 def modes_kernel(
-    total_rows, high_ref, low_hbm, w_ref, table_ref, resp_ref, out_ref, low_ref, a_ref, sem
+    total_rows, high_ref, low_hbm, w_ref, table_ref, resp_ref, out_ref, low_ref, a_ref, sems
 ):
     padded, cols = high_ref.shape
-    fetch_low = pltpu.make_async_copy(low_hbm, low_ref, sem)
-    fetch_low.start()
+    pieces = sems.shape[0]
+    fetches = []
+    for i in range(pieces):
+        first = padded // LANES * i // pieces * LANES
+        last = padded // LANES * (i + 1) // pieces * LANES
+        rows = pl.ds(first, last - first)
+        fetches.append(pltpu.make_async_copy(low_hbm.at[rows], low_ref.at[rows], sems.at[i]))
+    for fetch in fetches:
+        fetch.start()
     groups = RESP_ROWS // 2
     lane = lax.broadcasted_iota(jnp.int32, (RESP_ROWS, LANES), 1)
     left = lane < HALF
@@ -486,7 +522,8 @@
             a_ref[pl.ds(2 * NF + q * RESP_ROWS, RESP_ROWS), own] = low
     both = jnp.dot(a_ref[...], high_ref[...], preferred_element_type=jnp.float32)
     modes = both[: 2 * NF] + both[2 * NF :]
-    fetch_low.wait()
+    for fetch in fetches:
+        fetch.wait()
     modes += jnp.dot(
         a_ref[pl.ds(0, 2 * NF), :], low_ref[...], preferred_element_type=jnp.float32
     )
@@ -515,7 +552,7 @@
         scratch_shapes=[
             pltpu.VMEM((padded, cols), jnp.bfloat16),
             pltpu.VMEM((4 * NF, padded), jnp.bfloat16),
-            pltpu.SemaphoreType.DMA(()),
+            pltpu.SemaphoreType.DMA((4,)),
         ],
         compiler_params=pltpu.CompilerParams(vmem_limit_bytes=VMEM_LIMIT),
         cost_estimate=pl.CostEstimate(

time: 43.1 us -> 42.5 us (0.986)
  Pallas kernels: 16.4 us -> 15.8 us
    pallas_call x1, Pallas kernels: 10.6 us -> 10.1 us  [gram_parts(): pl.pallas_call(functools.partial(gram_kernel, total_rows, places, by_core...]
where the time goes in v2:
time: 42.5 us; the launch traced here: 42.2 us
  Pallas kernels  15.8 us (37%)
  blocking collectives  10.4 us (24%)
  waiting for transfers between devices  8.18 us (19%)
  starting transfers between devices  6.32 us (15%)
  other arithmetic  0.77 us (2%)
  between operations  0.7 us (2%)
    all_to_all x1, blocking collectives, direction_shards(): lax.all_to_all(parts, ('pts', 'freq'), 0, 0, axis_index_groups=near, tile...  10.4 us
    pallas_call x1, Pallas kernels, gram_parts(): pl.pallas_call(functools.partial(gram_kernel, total_rows, places, by_core...  10.1 us
    ppermute x6, waiting for transfers between devices, swap(): lax.ppermute(value, ('pts', 'freq'), [(i, i ^ mask) for i in range(n_devi...  8.18 us
    ppermute x6, starting transfers between devices, swap(): lax.ppermute(value, ('pts', 'freq'), [(i, i ^ mask) for i in range(n_devi...  6.32 us
    pallas_call x1, Pallas kernels, local_modes(): pl.pallas_call(functools.partial(modes_kernel, total_rows), out_shape=flo...  3.11 us
    pallas_call x7, Pallas kernels, call(): pl.pallas_call(kernel, out_shape=out_shape, in_specs=[VMEM] * len(args),...  2.65 us
  transfers between devices with their start and end apart: 6, of which 5 were waited for; matrix products, arithmetic and copies ran while one was open for 0% of the time, Pallas kernels for 11%

profile of v2, /device:TPU:0, one launch (start us, length us, event | category | flops | bytes accessed | tf_op | source)
XLA Modules:
  0.0 42.2 jit_solution(15580908110082454099)
XLA Ops:
  0.6 0.8 %select_maximum_fusion.aux_ref = f32[70,128]{1,0:T(8,128)S(1)} fusion(f32[64,64]{1,0:T(8,128)} %bitcast.8, f32[6,128]{1,0:T(8,128)} %bitcast.6), kind=kLoop, calls=%fused_computation.1 | loop fusion | flops 26880 | bytes 55296 | tf_op jit(solution)/shard_map/concatenate | solution.py:326
  1.4 0.0 copy-start
  1.4 0.0 copy-start.1
  1.4 10.1 %gram_parts.1 = (f32[288,128]{1,0:T(8,128)S(1)}, f32[288,128]{1,0:T(8,128)S(1)}, bf16[2176,384]{1,0:T(8,128)(2,1)S(1)}, bf16[2176,384]{1,0:T(8,128)(2,1)}) custom-call(f32[2112,384]{1,0:T(8,128)} %x_hbm.1, f32[70,128]{1,0:T(8,128)S(1)} %select_maximum_fusion.aux_ref), custom_call_target="tpu_custom_call" | custom-call | flops 5000000000 | bytes 8000000 | tf_op jit(solution)/shard_map/gram_parts/pallas_call | solution.py:331
  11.5 0.5 %collective-permute-start = (f32[288,128]{1,0:T(8,128)S(1)}, f32[288,128]{1,0:T(8,128)S(1)}, u32[]{:S(2)}, u32[]{:S(2)}) collective-permute-start(f32[288,128]{1,0:T(8,128)S(1)} %get-tuple-element.9), channel_id=1, source_target_pairs={{0,2},{1,3},{2,0},{3,1},{4,6},{5,7},{6,4},{7,5},{8,10},{9,11},{10,... | collective-permute-start | bytes 442376 | tf_op jit(solution)/shard_map/ppermute | solution.py:592
  12.0 1.0 %collective-permute-done.got_ref = f32[288,128]{1,0:T(8,128)S(1)} collective-permute-done((f32[288,128]{1,0:T(8,128)S(1)}, f32[288,128]{1,0:T(8,128)S(1)}, u32[]{:S(2)}, u32[]{:S(2)}) %collective-permute-start) | collective-permute-done | bytes 147488 | tf_op jit(solution)/shard_map/ppermute | solution.py:592
  13.0 10.4 %all_to_all.5.parts_ref = f32[4,96,128]{2,1,0:T(8,128)S(1)} all-to-all(f32[4,96,128]{2,1,0:T(8,128)S(1)} %add_core.1), channel_id=1, replica_groups={{0,1,4,5},{2,3,6,7},{8,9,12,13},{10,11,14,15},{16,17,20,21},{18,19,22,2..., dimensions={0} | all-to-all | bytes 393216 | tf_op jit(solution)/shard_map/all_to_all | solution.py:609
  23.5 1.6 %collective-permute-start.1 = (f32[96,128]{1,0:T(8,128)S(1)}, f32[96,128]{1,0:T(8,128)S(1)}, u32[]{:S(2)}, u32[]{:S(2)}) collective-permute-start(f32[96,128]{1,0:T(8,128)S(1)} %add_near.1.kept_ref), channel_id=1, source_target_pairs={{0,8},{1,9},{2,10},{3,11},{4,12},{5,13},{6,14},{7,15},{8,0},{9,1},... | collective-permute-start | bytes 147464 | tf_op jit(solution)/shard_map/ppermute | solution.py:592
  25.1 2.5 %collective-permute-done.1.got_ref = f32[96,128]{1,0:T(8,128)S(1)} collective-permute-done((f32[96,128]{1,0:T(8,128)S(1)}, f32[96,128]{1,0:T(8,128)S(1)}, u32[]{:S(2)}, u32[]{:S(2)}) %collective-permute-start.1) | collective-permute-done | bytes 49184 | tf_op jit(solution)/shard_map/ppermute | solution.py:592
  27.6 2.7 %collective-permute-start.2 = (f32[96,128]{1,0:T(8,128)S(1)}, f32[96,128]{1,0:T(8,128)S(1)}, u32[]{:S(2)}, u32[]{:S(2)}) collective-permute-start(f32[96,128]{1,0:T(8,128)S(1)} %add_z.1.kept_ref), channel_id=1, source_target_pairs={{0,16},{1,17},{2,18},{3,19},{4,20},{5,21},{6,22},{7,23},{8,24},{9,... | collective-permute-start | bytes 147464 | tf_op jit(solution)/shard_map/ppermute | solution.py:592
  30.3 2.4 %collective-permute-done.2.got_ref = f32[96,128]{1,0:T(8,128)S(1)} collective-permute-done((f32[96,128]{1,0:T(8,128)S(1)}, f32[96,128]{1,0:T(8,128)S(1)}, u32[]{:S(2)}, u32[]{:S(2)}) %collective-permute-start.2) | collective-permute-done | bytes 49184 | tf_op jit(solution)/shard_map/ppermute | solution.py:592
  32.7 0.1 finish.1
  32.8 0.8 %collective-permute-start.3 = (f32[64,128]{1,0:T(8,128)S(1)}, f32[64,128]{1,0:T(8,128)S(1)}, u32[]{:S(2)}, u32[]{:S(2)}) collective-permute-start(f32[64,128]{1,0:T(8,128)S(1)} %get-tuple-element.10.own_ref), channel_id=1, source_target_pairs={{0,4},{1,5},{2,6},{3,7},{4,0},{5,1},{6,2},{7,3},{8,12},{9,13},{10,... | collective-permute-start | bytes 98312 | tf_op jit(solution)/shard_map/ppermute | solution.py:592
  33.6 0.0 copy-done
  33.6 0.0 copy-done.1
  33.6 3.1 %local_modes.1.kept_ref = f32[2,6,32,128]{3,2,1,0:T(8,128)S(1)} custom-call(bf16[2176,384]{1,0:T(8,128)(2,1)S(1)} %get-tuple-element.11.high_ref, bf16[2176,384]{1,0:T(8,128)(2,1)} %get-tuple-element.12.low_hbm, f32[6,128]{1,0:T(8,128)S(1)} %bitcast.7, f32[2,128,128]{2,1,0:T(8,128)S(1)} %copy-done.1, f32[32,128]{1,0:T(8,128)S(1)} %get-tuple-element.13.resp_ref), custom_call_target="tpu_custom_call" | custom-call | flops 3000000000 | bytes 8000000 | tf_op jit(solution)/shard_map/local_modes/pallas_call | solution.py:547
  36.7 0.6 %collective-permute-start.5 = (f32[6,32,128]{2,1,0:T(8,128)S(1)}, f32[6,32,128]{2,1,0:T(8,128)S(1)}, u32[]{:S(2)}, u32[]{:S(2)}) collective-permute-start(f32[6,32,128]{2,1,0:T(8,128)S(1)} %slice_bitcast_fusion), channel_id=1, source_target_pairs={{0,1},{1,0},{2,3},{3,2},{4,5},{5,4},{6,7},{7,6},{8,9},{9,8},{10,11... | collective-permute-start | bytes 294920 | tf_op jit(solution)/shard_map/ppermute | solution.py:592
  37.4 0.0 collective-permute-done.3.got_ref
  37.4 0.1 collective-permute-start.4
  37.5 1.2 %collective-permute-done.4.refs_1_ = f32[128,128]{1,0:T(8,128)S(1)} collective-permute-done((f32[128,128]{1,0:T(8,128)S(1)}, f32[128,128]{1,0:T(8,128)S(1)}, u32[]{:S(2)}, u32[]{:S(2)}) %collective-permute-start.4) | collective-permute-done | bytes 65568 | tf_op jit(solution)/shard_map/ppermute | solution.py:592
  38.7 1.7 %unpack_gram.1 = f32[32,2,32,32]{3,2,1,0:T(8,128)} custom-call(f32[128,128]{1,0:T(8,128)S(1)} %join_y.1.refs_0_, f32[128,128]{1,0:T(8,128)S(1)} %collective-permute-done.4.refs_1_), custom_call_target="tpu_custom_call" | custom-call | tf_op jit(solution)/shard_map/unpack_gram/pallas_call | solution.py:381
  40.4 1.0 %collective-permute-done.5.got_ref = f32[6,32,128]{2,1,0:T(8,128)S(1)} collective-permute-done((f32[6,32,128]{2,1,0:T(8,128)S(1)}, f32[6,32,128]{2,1,0:T(8,128)S(1)}, u32[]{:S(2)}, u32[]{:S(2)}) %collective-permute-start.5) | collective-permute-done | bytes 98336 | tf_op jit(solution)/shard_map/ppermute | solution.py:592
  41.4 0.8 %join_modes.1 = f32[32,2,768]{2,1,0:T(2,128)} custom-call(f32[2,6,32,128]{3,2,1,0:T(8,128)S(1)} %local_modes.1.kept_ref, f32[6,32,128]{2,1,0:T(8,128)S(1)} %collective-permute-done.5.got_ref), custom_call_target="tpu_custom_call" | custom-call | tf_op jit(solution)/shard_map/join_modes/pallas_call | solution.py:381
  (5 shorter events, 0.1 us)
Async XLA Ops:
  1.4 32.2 %copy-start = (f32[768]{0:T(1024)S(1)}, f32[768]{0:T(1024)}, u32[]{:S(2)}) copy-start(f32[768]{0:T(1024)} %param.5) | copy-start | bytes 9220
  1.4 32.2 %copy-start.1 = (f32[2,128,128]{2,1,0:T(8,128)S(1)}, f32[2,128,128]{2,1,0:T(8,128)}, u32[]{:S(2)}) copy-start(f32[2,128,128]{2,1,0:T(8,128)} %constant.5.clone.table_ref) | copy-start | bytes 393220
  11.5 1.5 %collective-permute-start = (f32[288,128]{1,0:T(8,128)S(1)}, f32[288,128]{1,0:T(8,128)S(1)}, u32[]{:S(2)}, u32[]{:S(2)}) collective-permute-start(f32[288,128]{1,0:T(8,128)S(1)} %get-tuple-element.9), channel_id=1, source_target_pairs={{0,2},{1,3},{2,0},{3,1},{4,6},{5,7},{6,4},{7,5},{8,10},{9,11},{10,... | collective-permute-start | bytes 442376 | tf_op jit(solution)/shard_map/ppermute | solution.py:592
  23.5 4.2 %collective-permute-start.1 = (f32[96,128]{1,0:T(8,128)S(1)}, f32[96,128]{1,0:T(8,128)S(1)}, u32[]{:S(2)}, u32[]{:S(2)}) collective-permute-start(f32[96,128]{1,0:T(8,128)S(1)} %add_near.1.kept_ref), channel_id=1, source_target_pairs={{0,8},{1,9},{2,10},{3,11},{4,12},{5,13},{6,14},{7,15},{8,0},{9,1},... | collective-permute-start | bytes 147464 | tf_op jit(solution)/shard_map/ppermute | solution.py:592
  27.6 5.0 %collective-permute-start.2 = (f32[96,128]{1,0:T(8,128)S(1)}, f32[96,128]{1,0:T(8,128)S(1)}, u32[]{:S(2)}, u32[]{:S(2)}) collective-permute-start(f32[96,128]{1,0:T(8,128)S(1)} %add_z.1.kept_ref), channel_id=1, source_target_pairs={{0,16},{1,17},{2,18},{3,19},{4,20},{5,21},{6,22},{7,23},{8,24},{9,... | collective-permute-start | bytes 147464 | tf_op jit(solution)/shard_map/ppermute | solution.py:592
  32.8 4.6 %collective-permute-start.3 = (f32[64,128]{1,0:T(8,128)S(1)}, f32[64,128]{1,0:T(8,128)S(1)}, u32[]{:S(2)}, u32[]{:S(2)}) collective-permute-start(f32[64,128]{1,0:T(8,128)S(1)} %get-tuple-element.10.own_ref), channel_id=1, source_target_pairs={{0,4},{1,5},{2,6},{3,7},{4,0},{5,1},{6,2},{7,3},{8,12},{9,13},{10,... | collective-permute-start | bytes 98312 | tf_op jit(solution)/shard_map/ppermute | solution.py:592
  36.7 4.7 %collective-permute-start.5 = (f32[6,32,128]{2,1,0:T(8,128)S(1)}, f32[6,32,128]{2,1,0:T(8,128)S(1)}, u32[]{:S(2)}, u32[]{:S(2)}) collective-permute-start(f32[6,32,128]{2,1,0:T(8,128)S(1)} %slice_bitcast_fusion), channel_id=1, source_target_pairs={{0,1},{1,0},{2,3},{3,2},{4,5},{5,4},{6,7},{7,6},{8,9},{9,8},{10,11... | collective-permute-start | bytes 294920 | tf_op jit(solution)/shard_map/ppermute | solution.py:592
  37.4 1.3 %collective-permute-start.4 = (f32[128,128]{1,0:T(8,128)S(1)}, f32[128,128]{1,0:T(8,128)S(1)}, u32[]{:S(2)}, u32[]{:S(2)}) collective-permute-start(f32[128,128]{1,0:T(8,128)S(1)} %join_y.1.refs_0_), channel_id=1, source_target_pairs={{0,2},{1,3},{2,0},{3,1},{4,6},{5,7},{6,4},{7,5},{8,10},{9,11},{10,... | collective-permute-start | bytes 196616 | tf_op jit(solution)/shard_map/ppermute | solution.py:592

commit v3 on v2

--- a/solution.py
+++ b/solution.py
@@ -33,6 +33,11 @@
     high = table.astype(jnp.bfloat16)
     low = (table - high.astype(np.float64)).astype(jnp.bfloat16)
     return high, low
+
+
+def window_leaks():
+    real, _ = dft_values()
+    return [float(np.sum(real[k])) for k in range(2)]
 
 
 def mode_tables():
@@ -156,6 +161,7 @@
     keep_ref,
     send_ref,
     high_ref,
+    rest_ref,
     low_hbm,
     x_ref,
     dft_ref,
@@ -173,44 +179,37 @@
     out_sem,
 ):
     times, cols = x_ref.shape
-    halves = times // HALF
     col_tiles = cols // LANES
     block_refs = (block_even, block_odd)
-    pieces = in_sems.shape[0]
-    piece = times // pieces
-
-    def fetch(i):
-        rows = pl.ds(i * piece, piece)
-        return pltpu.make_async_copy(x_hbm.at[rows], x_ref.at[rows], in_sems.at[i])
-
-    for i in range(pieces):
-        fetch(i).start()
+    cuts = [0] + [(first + TILE + 1) * HALF for first in range(0, NB, TILE)]
+
+    def fetches(i):
+        middle = (cuts[i] + cuts[i + 1]) // (2 * HALF) * HALF
+        for n, (first, last) in enumerate(((cuts[i], middle), (middle, cuts[i + 1]))):
+            rows = pl.ds(first, last - first)
+            yield pltpu.make_async_copy(x_hbm.at[rows], x_ref.at[rows], in_sems.at[2 * i + n])
+
+    for i in range(len(cuts) - 1):
+        for fetch in fetches(i):
+            fetch.start()
     fill_dft(dft_ref)
     spread_start(aux_ref, spread_ref)
-
-    acc = jnp.zeros((HALF, cols), jnp.float32)
-    for i in range(pieces):
-        fetch(i).wait()
-        for h in range(piece // HALF):
-            acc = acc + x_ref[pl.ds(i * piece + h * HALF, HALF), :]
-    mean = jnp.sum(acc, axis=0, keepdims=True) / times
     weights = load_weights(aux_ref.at[pl.ds(2 * NB, aux_ref.shape[0] - 2 * NB)], col_tiles)
     scale = jnp.sqrt(weights / (2.0 * total_rows))
-
-    def center(i, carry):
-        rows = pl.ds(pl.multiple_of(i * HALF, HALF), HALF)
-        high, low = split((x_ref[rows, :] - mean) * scale)
-        high_ref[rows, :] = high
-        low_ref[rows, :] = low
-        return carry
-
-    lax.fori_loop(0, halves, center, 0, unroll=3)
-    pad = high_ref.shape[0] - times
-    if pad:
-        high_ref[pl.ds(times, pad), :] = jnp.zeros((pad, cols), jnp.bfloat16)
-        low_ref[pl.ds(times, pad), :] = jnp.zeros((pad, cols), jnp.bfloat16)
-    save_low = pltpu.make_async_copy(low_ref, low_hbm, out_sem)
-    save_low.start()
+    for fetch in fetches(0):
+        fetch.wait()
+    first_mean = jnp.mean(x_ref[pl.ds(0, NFFT), :], axis=0, keepdims=True)
+
+    def center(i, acc):
+        def step(h, acc):
+            rows = pl.ds(pl.multiple_of(h * HALF, HALF), HALF)
+            value = x_ref[rows, :] - first_mean
+            high, low = split(value * scale)
+            high_ref[rows, :] = high
+            low_ref[rows, :] = low
+            return acc + value
+
+        return lax.fori_loop(cuts[i] // HALF, cuts[i + 1] // HALF, step, acc, unroll=True)
 
     def transform(first):
         for i in range(TILE // 2):
@@ -235,11 +234,27 @@
                 for k in range(TILE):
                     spec_ref[c, o * TILE + k, pl.ds(first, TILE), :] = tiles[k]
 
+    acc = center(0, jnp.zeros((HALF, cols), jnp.float32))
     transform(0)
     for first in range(0, NB, TILE):
         if first + TILE < NB:
+            for fetch in fetches(first // TILE + 1):
+                fetch.wait()
+            acc = center(first // TILE + 1, acc)
             transform(first + TILE)
         arrange(first)
+    pad = high_ref.shape[0] - times
+    if pad:
+        high_ref[pl.ds(times, pad), :] = jnp.zeros((pad, cols), jnp.bfloat16)
+        low_ref[pl.ds(times, pad), :] = jnp.zeros((pad, cols), jnp.bfloat16)
+    save_low = pltpu.make_async_copy(low_ref, low_hbm, out_sem)
+    save_low.start()
+    rest = jnp.sum(acc, axis=0, keepdims=True) / times * scale
+    rest_ref[...] = jnp.broadcast_to(rest, rest_ref.shape)
+    for k, leak in enumerate(window_leaks()):
+        for c in range(col_tiles):
+            part = rest[:, c * LANES : (c + 1) * LANES]
+            spec_ref[c, k] = spec_ref[c, k] - leak * part
 
     row = lax.broadcasted_iota(jnp.int32, (NB, LANES), 0)
     lane = lax.broadcasted_iota(jnp.int32, (NB, LANES), 1)
@@ -324,15 +339,14 @@
     start = jnp.transpose(start_vec, (1, 2, 0)).reshape(2 * NB, NF)
     start = jnp.pad(start, ((0, 0), (0, LANES - NF)))
     aux = jnp.concatenate([start, weight_rows], axis=0)
-    pieces = 11
     any_space = pl.BlockSpec(memory_space=pl.ANY)
     saved = jax.ShapeDtypeStruct((-(-times // LANES) * LANES, cols), jnp.bfloat16)
     half = floats(NF // 4 * NB // 2 + RESP_ROWS, LANES)
     return pl.pallas_call(
         functools.partial(gram_kernel, total_rows, places, by_core),
-        out_shape=(half, half, saved, saved),
+        out_shape=(half, half, saved, floats(8, cols), saved),
         in_specs=[any_space, VMEM],
-        out_specs=(VMEM, VMEM, VMEM, any_space),
+        out_specs=(VMEM, VMEM, VMEM, VMEM, any_space),
         scratch_shapes=[
             pltpu.VMEM((times, cols), jnp.float32),
             pltpu.VMEM((4 * NF, 2 * NFFT), jnp.bfloat16),
@@ -346,7 +360,7 @@
             pltpu.VMEM((NF // PACK, NB, LANES), jnp.float32),
             pltpu.VMEM((NF // PACK, 2 * NB, LANES), jnp.float32),
             pltpu.VMEM((NF // 2 * NB // 2 + RESP_ROWS, LANES), jnp.float32),
-            pltpu.SemaphoreType.DMA((pieces,)),
+            pltpu.SemaphoreType.DMA((2 * NB // TILE,)),
             pltpu.SemaphoreType.DMA(()),
         ],
         compiler_params=pltpu.CompilerParams(vmem_limit_bytes=VMEM_LIMIT),
@@ -477,7 +491,7 @@
 
 
 def modes_kernel(
-    total_rows, high_ref, low_hbm, w_ref, table_ref, resp_ref, out_ref, low_ref, a_ref, sems
+    total_rows, high_ref, low_hbm, rest_ref, w_ref, table_ref, resp_ref, out_ref, low_ref, a_ref, sems
 ):
     padded, cols = high_ref.shape
     pieces = sems.shape[0]
@@ -489,6 +503,9 @@
         fetches.append(pltpu.make_async_copy(low_hbm.at[rows], low_ref.at[rows], sems.at[i]))
     for fetch in fetches:
         fetch.start()
+    row = lax.broadcasted_iota(jnp.int32, (RESP_ROWS, 1), 0)
+    leaks = window_leaks()
+    corrections = []
     groups = RESP_ROWS // 2
     lane = lax.broadcasted_iota(jnp.int32, (RESP_ROWS, LANES), 1)
     left = lane < HALF
@@ -496,6 +513,11 @@
         resp = resp_ref[...]
         if q:
             resp = pltpu.roll(resp, LANES - q * NB, 1)
+        if q < len(leaks):
+            total = jnp.sum(jnp.where(lane < NB, resp, 0.0), axis=1, keepdims=True) * leaks[q]
+            corrections.append(jnp.where(row % groups == 0, total, 0.0) * rest_ref[pl.ds(0, 1), :])
+        else:
+            corrections.append(jnp.zeros((RESP_ROWS, cols), jnp.float32))
         real = jnp.concatenate([resp[:groups]] * 2, axis=0)
         imag = jnp.concatenate([resp[groups:]] * 2, axis=0)
         rows = pl.ds(q * RESP_ROWS, RESP_ROWS)
@@ -522,6 +544,7 @@
             a_ref[pl.ds(2 * NF + q * RESP_ROWS, RESP_ROWS), own] = low
     both = jnp.dot(a_ref[...], high_ref[...], preferred_element_type=jnp.float32)
     modes = both[: 2 * NF] + both[2 * NF :]
+    modes -= jnp.concatenate(corrections, axis=0)
     for fetch in fetches:
         fetch.wait()
     modes += jnp.dot(
@@ -542,12 +565,12 @@
                     ]
 
 
-def local_modes(high, low, weight_rows, response, total_rows, n_freq):
+def local_modes(high, low, rest, weight_rows, response, total_rows, n_freq):
     padded, cols = high.shape
     return pl.pallas_call(
         functools.partial(modes_kernel, total_rows),
         out_shape=floats(n_freq, 2 * cols // LANES, NF // n_freq, LANES),
-        in_specs=[VMEM, pl.BlockSpec(memory_space=pl.ANY)] + [VMEM] * 3,
+        in_specs=[VMEM, pl.BlockSpec(memory_space=pl.ANY)] + [VMEM] * 4,
         out_specs=VMEM,
         scratch_shapes=[
             pltpu.VMEM((padded, cols), jnp.bfloat16),
@@ -559,7 +582,7 @@
             flops=3_000_000_000, bytes_accessed=8_000_000, transcendentals=0
         ),
         name="local_modes",
-    )(high, low, weight_rows, jnp.asarray(mode_tables()), response)
+    )(high, low, rest, weight_rows, jnp.asarray(mode_tables()), response)
 
 
 def join_kernel(kept_ref, got_ref, out_ref):
@@ -602,7 +625,7 @@
     places = [
         (i // 8 % 2) * 16 + (i // 4 % 2) * 8 + (i // 16) * 4 + i % 4 for i in range(NF // 2)
     ]
-    keep, send, high, low = gram_parts(
+    keep, send, high, rest, low = gram_parts(
         snapshots, weight_rows, start_vec, total_rows, places, True
     )
     parts = add_core(keep, swap(send, core))
@@ -613,7 +636,7 @@
     part = add("add_z", part, swap(part, z_near))
     packed, response = finish(part, swap(part, z_far))
     other = swap(packed, y)
-    modes = local_modes(high, low, weight_rows, response, total_rows, 2)
+    modes = local_modes(high, low, rest, weight_rows, response, total_rows, 2)
     packed = small_call(join_y_kernel, "join_y", floats(2 * packed.shape[0], LANES))(packed, other)
     gram_mine = unpack_gram(packed, swap(packed, core))
     return gram_mine, join_modes(modes, swap(modes[1], x))
@@ -627,7 +650,7 @@
     group = lax.axis_index("freq")
     weight_rows = weight.reshape(-1, LANES)
     places = list(range(NF // 2))
-    first, second, high, low = gram_parts(
+    first, second, high, rest, low = gram_parts(
         snapshots, weight_rows, start_vec, total_rows, places, False
     )
     parts = jnp.concatenate([first[:-RESP_ROWS], second[:-RESP_ROWS]], axis=0)
@@ -639,7 +662,7 @@
     response = lax.all_gather(response_of(gram_mine, start_mine), "freq", axis=0, tiled=True)
     response = jnp.transpose(response.reshape(NF // PACK, PACK, 2, NB), (2, 0, 1, 3))
     response = response.reshape(RESP_ROWS, LANES)
-    modes = local_modes(high, low, weight_rows, response, total_rows, n_freq)
+    modes = local_modes(high, low, rest, weight_rows, response, total_rows, n_freq)
     modes = lax.all_to_all(modes, "freq", 0, 0, tiled=True)
     modes = modes.reshape(n_freq, cols // LANES, 2, mine_count, LANES)
     modes = jnp.transpose(modes, (3, 2, 0, 1, 4)).reshape(mine_count, 2, n_freq * cols)

time: 42.5 us -> 42.1 us (level)
    pallas_call x1, Pallas kernels: 10.1 us -> 9.63 us  [gram_parts(): pl.pallas_call(functools.partial(gram_kernel, total_rows, places, by_core...]
  transfers between devices with their start and end apart: 6 -> 6, of which waited for: 5 -> 5; matrix products, arithmetic and copies ran while one was open for 0% -> 0% of each run, Pallas kernels for 11% -> 12%
where the time goes in v3:
time: 42.1 us; the launch traced here: 41.8 us
  Pallas kernels  15.4 us (37%)
  blocking collectives  10.4 us (25%)
  waiting for transfers between devices  8.18 us (19%)
  starting transfers between devices  6.31 us (15%)
  other arithmetic  0.77 us (2%)
  between operations  0.7 us (2%)
    all_to_all x1, blocking collectives, direction_shards(): lax.all_to_all(parts, ('pts', 'freq'), 0, 0, axis_index_groups=near, tile...  10.4 us
    pallas_call x1, Pallas kernels, gram_parts(): pl.pallas_call(functools.partial(gram_kernel, total_rows, places, by_core...  9.63 us
    ppermute x6, waiting for transfers between devices, swap(): lax.ppermute(value, ('pts', 'freq'), [(i, i ^ mask) for i in range(n_devi...  8.18 us
    ppermute x6, starting transfers between devices, swap(): lax.ppermute(value, ('pts', 'freq'), [(i, i ^ mask) for i in range(n_devi...  6.31 us
    pallas_call x1, Pallas kernels, local_modes(): pl.pallas_call(functools.partial(modes_kernel, total_rows), out_shape=flo...  3.12 us
    pallas_call x7, Pallas kernels, call(): pl.pallas_call(kernel, out_shape=out_shape, in_specs=[VMEM] * len(args),...  2.65 us
  transfers between devices with their start and end apart: 6, of which 5 were waited for; matrix products, arithmetic and copies ran while one was open for 0% of the time, Pallas kernels for 12%

profile of v3, /device:TPU:0, one launch (start us, length us, event | category | flops | bytes accessed | tf_op | source)
XLA Modules:
  0.0 41.8 jit_solution(5848422487925404269)
XLA Ops:
  0.6 0.8 %select_maximum_fusion.aux_ref = f32[70,128]{1,0:T(8,128)S(1)} fusion(f32[64,64]{1,0:T(8,128)} %bitcast.8, f32[6,128]{1,0:T(8,128)} %bitcast.6), kind=kLoop, calls=%fused_computation.1 | loop fusion | flops 26880 | bytes 55296 | tf_op jit(solution)/shard_map/concatenate | solution.py:341
  1.4 0.0 copy-start
  1.4 0.0 copy-start.1
  1.4 9.6 %gram_parts.1 = (f32[288,128]{1,0:T(8,128)S(1)}, f32[288,128]{1,0:T(8,128)S(1)}, bf16[2176,384]{1,0:T(8,128)(2,1)S(1)}, f32[8,384]{1,0:T(8,128)S(1)}, bf16[2176,384]{1,0:T(8,128)(2,1)}) custom-call(f32[2112,384]{1,0:T(8,128)} %x_hbm.1, f32[70,128]{1,0:T(8,128)S(1)} %select_maximum_fusion.aux_ref), custom_call_target="tpu_custom_call" | custom-call | flops 5000000000 | bytes 8000000 | tf_op jit(solution)/shard_map/gram_parts/pallas_call | solution.py:345
  11.1 0.5 %collective-permute-start = (f32[288,128]{1,0:T(8,128)S(1)}, f32[288,128]{1,0:T(8,128)S(1)}, u32[]{:S(2)}, u32[]{:S(2)}) collective-permute-start(f32[288,128]{1,0:T(8,128)S(1)} %get-tuple-element.10), channel_id=1, source_target_pairs={{0,2},{1,3},{2,0},{3,1},{4,6},{5,7},{6,4},{7,5},{8,10},{9,11},{10,... | collective-permute-start | bytes 442376 | tf_op jit(solution)/shard_map/ppermute | solution.py:615
  11.6 1.0 %collective-permute-done.got_ref = f32[288,128]{1,0:T(8,128)S(1)} collective-permute-done((f32[288,128]{1,0:T(8,128)S(1)}, f32[288,128]{1,0:T(8,128)S(1)}, u32[]{:S(2)}, u32[]{:S(2)}) %collective-permute-start) | collective-permute-done | bytes 147488 | tf_op jit(solution)/shard_map/ppermute | solution.py:615
  12.6 10.4 %all_to_all.5.parts_ref = f32[4,96,128]{2,1,0:T(8,128)S(1)} all-to-all(f32[4,96,128]{2,1,0:T(8,128)S(1)} %add_core.1), channel_id=1, replica_groups={{0,1,4,5},{2,3,6,7},{8,9,12,13},{10,11,14,15},{16,17,20,21},{18,19,22,2..., dimensions={0} | all-to-all | bytes 393216 | tf_op jit(solution)/shard_map/all_to_all | solution.py:632
  23.0 1.6 %collective-permute-start.1 = (f32[96,128]{1,0:T(8,128)S(1)}, f32[96,128]{1,0:T(8,128)S(1)}, u32[]{:S(2)}, u32[]{:S(2)}) collective-permute-start(f32[96,128]{1,0:T(8,128)S(1)} %add_near.1.kept_ref), channel_id=1, source_target_pairs={{0,8},{1,9},{2,10},{3,11},{4,12},{5,13},{6,14},{7,15},{8,0},{9,1},... | collective-permute-start | bytes 147464 | tf_op jit(solution)/shard_map/ppermute | solution.py:615
  24.7 2.5 %collective-permute-done.1.got_ref = f32[96,128]{1,0:T(8,128)S(1)} collective-permute-done((f32[96,128]{1,0:T(8,128)S(1)}, f32[96,128]{1,0:T(8,128)S(1)}, u32[]{:S(2)}, u32[]{:S(2)}) %collective-permute-start.1) | collective-permute-done | bytes 49184 | tf_op jit(solution)/shard_map/ppermute | solution.py:615
  27.2 2.7 %collective-permute-start.2 = (f32[96,128]{1,0:T(8,128)S(1)}, f32[96,128]{1,0:T(8,128)S(1)}, u32[]{:S(2)}, u32[]{:S(2)}) collective-permute-start(f32[96,128]{1,0:T(8,128)S(1)} %add_z.1.kept_ref), channel_id=1, source_target_pairs={{0,16},{1,17},{2,18},{3,19},{4,20},{5,21},{6,22},{7,23},{8,24},{9,... | collective-permute-start | bytes 147464 | tf_op jit(solution)/shard_map/ppermute | solution.py:615
  29.9 2.4 %collective-permute-done.2.got_ref = f32[96,128]{1,0:T(8,128)S(1)} collective-permute-done((f32[96,128]{1,0:T(8,128)S(1)}, f32[96,128]{1,0:T(8,128)S(1)}, u32[]{:S(2)}, u32[]{:S(2)}) %collective-permute-start.2) | collective-permute-done | bytes 49184 | tf_op jit(solution)/shard_map/ppermute | solution.py:615
  32.3 0.1 finish.1
  32.4 0.8 %collective-permute-start.3 = (f32[64,128]{1,0:T(8,128)S(1)}, f32[64,128]{1,0:T(8,128)S(1)}, u32[]{:S(2)}, u32[]{:S(2)}) collective-permute-start(f32[64,128]{1,0:T(8,128)S(1)} %get-tuple-element.11.own_ref), channel_id=1, source_target_pairs={{0,4},{1,5},{2,6},{3,7},{4,0},{5,1},{6,2},{7,3},{8,12},{9,13},{10,... | collective-permute-start | bytes 98312 | tf_op jit(solution)/shard_map/ppermute | solution.py:615
  33.2 0.0 copy-done
  33.2 0.0 copy-done.1
  33.2 3.1 %local_modes.1.kept_ref = f32[2,6,32,128]{3,2,1,0:T(8,128)S(1)} custom-call(bf16[2176,384]{1,0:T(8,128)(2,1)S(1)} %get-tuple-element.12.high_ref, bf16[2176,384]{1,0:T(8,128)(2,1)} %get-tuple-element.13.low_hbm, f32[8,384]{1,0:T(8,128)S(1)} %get-tuple-element.14.rest_ref, f32[6,128]{1,0:T(8,128)S(1)} %bitcast.7, f32[2,128,128]{2,1,0:T(8,128)S(1)} %copy-done.1, ...), custom_call_target="tpu_custom_call" | custom-call | flops 3000000000 | bytes 8000000 | tf_op jit(solution)/shard_map/local_modes/pallas_call | solution.py:570
  36.3 0.6 %collective-permute-start.5 = (f32[6,32,128]{2,1,0:T(8,128)S(1)}, f32[6,32,128]{2,1,0:T(8,128)S(1)}, u32[]{:S(2)}, u32[]{:S(2)}) collective-permute-start(f32[6,32,128]{2,1,0:T(8,128)S(1)} %slice_bitcast_fusion), channel_id=1, source_target_pairs={{0,1},{1,0},{2,3},{3,2},{4,5},{5,4},{6,7},{7,6},{8,9},{9,8},{10,11... | collective-permute-start | bytes 294920 | tf_op jit(solution)/shard_map/ppermute | solution.py:615
  36.9 0.0 collective-permute-done.3.got_ref
  37.0 0.1 collective-permute-start.4
  37.0 1.2 %collective-permute-done.4.refs_1_ = f32[128,128]{1,0:T(8,128)S(1)} collective-permute-done((f32[128,128]{1,0:T(8,128)S(1)}, f32[128,128]{1,0:T(8,128)S(1)}, u32[]{:S(2)}, u32[]{:S(2)}) %collective-permute-start.4) | collective-permute-done | bytes 65568 | tf_op jit(solution)/shard_map/ppermute | solution.py:615
  38.3 1.7 %unpack_gram.1 = f32[32,2,32,32]{3,2,1,0:T(8,128)} custom-call(f32[128,128]{1,0:T(8,128)S(1)} %join_y.1.refs_0_, f32[128,128]{1,0:T(8,128)S(1)} %collective-permute-done.4.refs_1_), custom_call_target="tpu_custom_call" | custom-call | tf_op jit(solution)/shard_map/unpack_gram/pallas_call | solution.py:395
  40.0 1.0 %collective-permute-done.5.got_ref = f32[6,32,128]{2,1,0:T(8,128)S(1)} collective-permute-done((f32[6,32,128]{2,1,0:T(8,128)S(1)}, f32[6,32,128]{2,1,0:T(8,128)S(1)}, u32[]{:S(2)}, u32[]{:S(2)}) %collective-permute-start.5) | collective-permute-done | bytes 98336 | tf_op jit(solution)/shard_map/ppermute | solution.py:615
  41.0 0.8 %join_modes.1 = f32[32,2,768]{2,1,0:T(2,128)} custom-call(f32[2,6,32,128]{3,2,1,0:T(8,128)S(1)} %local_modes.1.kept_ref, f32[6,32,128]{2,1,0:T(8,128)S(1)} %collective-permute-done.5.got_ref), custom_call_target="tpu_custom_call" | custom-call | tf_op jit(solution)/shard_map/join_modes/pallas_call | solution.py:395
  (5 shorter events, 0.1 us)
Async XLA Ops:
  1.4 31.8 %copy-start = (f32[768]{0:T(1024)S(1)}, f32[768]{0:T(1024)}, u32[]{:S(2)}) copy-start(f32[768]{0:T(1024)} %param.5) | copy-start | bytes 9220
  1.4 31.8 %copy-start.1 = (f32[2,128,128]{2,1,0:T(8,128)S(1)}, f32[2,128,128]{2,1,0:T(8,128)}, u32[]{:S(2)}) copy-start(f32[2,128,128]{2,1,0:T(8,128)} %constant.5.clone.table_ref) | copy-start | bytes 393220
  11.1 1.5 %collective-permute-start = (f32[288,128]{1,0:T(8,128)S(1)}, f32[288,128]{1,0:T(8,128)S(1)}, u32[]{:S(2)}, u32[]{:S(2)}) collective-permute-start(f32[288,128]{1,0:T(8,128)S(1)} %get-tuple-element.10), channel_id=1, source_target_pairs={{0,2},{1,3},{2,0},{3,1},{4,6},{5,7},{6,4},{7,5},{8,10},{9,11},{10,... | collective-permute-start | bytes 442376 | tf_op jit(solution)/shard_map/ppermute | solution.py:615
  23.0 4.2 %collective-permute-start.1 = (f32[96,128]{1,0:T(8,128)S(1)}, f32[96,128]{1,0:T(8,128)S(1)}, u32[]{:S(2)}, u32[]{:S(2)}) collective-permute-start(f32[96,128]{1,0:T(8,128)S(1)} %add_near.1.kept_ref), channel_id=1, source_target_pairs={{0,8},{1,9},{2,10},{3,11},{4,12},{5,13},{6,14},{7,15},{8,0},{9,1},... | collective-permute-start | bytes 147464 | tf_op jit(solution)/shard_map/ppermute | solution.py:615
  27.2 5.0 %collective-permute-start.2 = (f32[96,128]{1,0:T(8,128)S(1)}, f32[96,128]{1,0:T(8,128)S(1)}, u32[]{:S(2)}, u32[]{:S(2)}) collective-permute-start(f32[96,128]{1,0:T(8,128)S(1)} %add_z.1.kept_ref), channel_id=1, source_target_pairs={{0,16},{1,17},{2,18},{3,19},{4,20},{5,21},{6,22},{7,23},{8,24},{9,... | collective-permute-start | bytes 147464 | tf_op jit(solution)/shard_map/ppermute | solution.py:615
  32.4 4.6 %collective-permute-start.3 = (f32[64,128]{1,0:T(8,128)S(1)}, f32[64,128]{1,0:T(8,128)S(1)}, u32[]{:S(2)}, u32[]{:S(2)}) collective-permute-start(f32[64,128]{1,0:T(8,128)S(1)} %get-tuple-element.11.own_ref), channel_id=1, source_target_pairs={{0,4},{1,5},{2,6},{3,7},{4,0},{5,1},{6,2},{7,3},{8,12},{9,13},{10,... | collective-permute-start | bytes 98312 | tf_op jit(solution)/shard_map/ppermute | solution.py:615
  36.3 4.7 %collective-permute-start.5 = (f32[6,32,128]{2,1,0:T(8,128)S(1)}, f32[6,32,128]{2,1,0:T(8,128)S(1)}, u32[]{:S(2)}, u32[]{:S(2)}) collective-permute-start(f32[6,32,128]{2,1,0:T(8,128)S(1)} %slice_bitcast_fusion), channel_id=1, source_target_pairs={{0,1},{1,0},{2,3},{3,2},{4,5},{5,4},{6,7},{7,6},{8,9},{9,8},{10,11... | collective-permute-start | bytes 294920 | tf_op jit(solution)/shard_map/ppermute | solution.py:615
  37.0 1.3 %collective-permute-start.4 = (f32[128,128]{1,0:T(8,128)S(1)}, f32[128,128]{1,0:T(8,128)S(1)}, u32[]{:S(2)}, u32[]{:S(2)}) collective-permute-start(f32[128,128]{1,0:T(8,128)S(1)} %join_y.1.refs_0_), channel_id=1, source_target_pairs={{0,2},{1,3},{2,0},{3,1},{4,6},{5,7},{6,4},{7,5},{8,10},{9,11},{10,... | collective-permute-start | bytes 196616 | tf_op jit(solution)/shard_map/ppermute | solution.py:615
